TPU v7x, 512 devices: a whole 4x8x8 slice. The times are simulated.
512 devices in a mesh: fiber: 512 (over y, x, z, core).
Axes of the slice: x: 4, y: 8, z: 8, core: 2. Of those that a mesh axis runs over, the one named last changes fastest.
Arguments:
- traces: float32 [16384, 3000], P('fiber'), may hold values from -16 to 16
- live: int32 [16384], P('fiber'), may hold values 0 or 1
- segment: int32 [16384], P('fiber'), may hold values from 0 to 340, never falling along the last dimension, each value on 1 to 96 neighbouring positions
Outputs:
- correlations: bfloat16 [16384, 128, 256], P('fiber')
Inputs may be any that keep to these rules, and one draw needn't show every extreme that they name: `live`: 1 marks a working channel. segment numbers never fall along the fiber, and a segment holds 1 to 96 channels.
All inputs are finite; a program needn't handle non-finite values. No bound on the sum of `live` on one device may be relied on, other than what follows from the above.
Results may differ from a plain program's by a relative error of at most 0.0071.
Values may be sent and summed in bfloat16 or wider, within the bound.
A program may use at most 64 MiB of HBM per device.

v0:
```python
import math

import jax
import jax.numpy as jnp
from jax import lax
from jax.sharding import PartitionSpec as P

LOW_BIN = 32
FB = 768
BAND = 64
HALF_WIN = 15
REACH = 4
LAGS = 256


span_width = 128
group_rows = 16
whiten_eps = 1.0


def with_halo(block, sides, width):
    for axis, dim in sides:
        count = lax.axis_size(axis)
        forward = [(i, i + 1) for i in range(count - 1)]
        backward = [(target, source) for source, target in forward]
        low = lax.ppermute(
            lax.slice_in_dim(block, block.shape[dim] - width, None, axis=dim), axis, forward
        )
        high = lax.ppermute(lax.slice_in_dim(block, 0, width, axis=dim), axis, backward)
        block = jnp.concatenate([low, block, high], axis=dim)
    return block


def shifted(value, axis, steps):
    count = lax.axis_size(axis)
    leading, last = (max(0, -steps), min(count, count - steps))
    return lax.ppermute(value, axis, [(source, source + steps) for source in range(leading, last)])


def lag_weights(length_total):
    bin_index = LOW_BIN + jnp.arange(FB, dtype=jnp.int32)
    lag_index = jnp.arange(LAGS, dtype=jnp.int32) - LAGS // 2
    phases = jnp.mod(bin_index[:, None] * lag_index[None, :], length_total).astype(jnp.float32) * (
        2.0 * math.pi / length_total
    )
    scaled = jnp.concatenate([jnp.cos(phases), -jnp.sin(phases)], axis=0) / math.sqrt(FB)
    return scaled.astype(jnp.bfloat16)


def spectrum(filtered, length_total):
    channels = filtered.shape[0]
    spans = -(-length_total // span_width)
    padded = jnp.pad(filtered, ((0, 0), (0, spans * span_width - filtered.shape[1])))
    bin_index = LOW_BIN + jnp.arange(FB, dtype=jnp.int32)
    taper = jnp.sin(math.pi * (jnp.arange(FB, dtype=jnp.float32) + 0.5) / FB)
    step_index = jnp.arange(span_width, dtype=jnp.int32)
    phases = jnp.mod(step_index[:, None] * bin_index[None, :], length_total).astype(jnp.float32) * (
        2.0 * math.pi / length_total
    )
    base = jnp.concatenate([jnp.cos(phases), -jnp.sin(phases)], axis=1)

    def add_span(counter, running):
        run_real, run_imag = running
        first = counter * span_width
        window = lax.dynamic_slice_in_dim(padded, first, span_width, 1)
        part = jnp.dot(
            window, base, precision=lax.Precision.HIGHEST, preferred_element_type=jnp.float32
        )
        part_real = part[:, :FB]
        part_imag = part[:, FB:]
        turn = jnp.mod(first * bin_index, length_total).astype(jnp.float32) * (
            2.0 * math.pi / length_total
        )
        cosine = jnp.cos(turn)
        sine = -jnp.sin(turn)
        return (
            run_real + part_real * cosine - part_imag * sine,
            run_imag + part_real * sine + part_imag * cosine,
        )

    empty = jnp.zeros((channels, FB), jnp.float32)
    run_real, run_imag = lax.fori_loop(0, spans, add_span, (empty, empty))
    return jnp.concatenate([run_real * taper, run_imag * taper], axis=1)


def correlate_block(whitened, partner_rows, table):
    channels = whitened.shape[0]
    partners = partner_rows.shape[0]
    grouped = whitened.reshape(channels // group_rows, group_rows, 2 * FB)
    partner_real = partner_rows[None, :, :FB].astype(jnp.float32)
    partner_imag = partner_rows[None, :, FB:].astype(jnp.float32)

    def one_group(rows_here):
        own_real = rows_here[:, None, :FB].astype(jnp.float32)
        own_imag = rows_here[:, None, FB:].astype(jnp.float32)
        real_cross = (own_real * partner_real + own_imag * partner_imag).astype(jnp.bfloat16)
        imag_cross = (own_imag * partner_real - own_real * partner_imag).astype(jnp.bfloat16)
        cross = jnp.concatenate([real_cross, imag_cross], axis=2).reshape(
            group_rows * partners, 2 * FB
        )
        result = jnp.dot(cross, table, preferred_element_type=jnp.float32)
        return result.astype(jnp.bfloat16).reshape(group_rows, partners, LAGS)

    return lax.map(one_group, grouped).reshape(channels, partners, LAGS)


def on_device(traces, live, segment):
    channels = traces.shape[0]
    length_total = traces.shape[1]
    labels = segment * 2 + live
    wide_labels = with_halo(labels, (("fiber", 0),), HALF_WIN)
    wide_live = wide_labels % 2
    wide_segment = wide_labels // 2
    target = jnp.arange(channels, dtype=jnp.int32)[:, None] + HALF_WIN
    source = jnp.arange(channels + 2 * HALF_WIN, dtype=jnp.int32)[None, :]
    inside = (
        (jnp.abs(source - target) <= HALF_WIN)
        & (wide_segment[None, :] == segment[:, None])
        & (wide_live[None, :] == 1)
    )
    counted = jnp.sum(inside.astype(jnp.int32), axis=1)
    divisor = jnp.maximum(counted, 1).astype(jnp.float32)[:, None]
    live_here = live.astype(jnp.float32)[:, None]
    widened = with_halo(traces, (("fiber", 0),), HALF_WIN)
    masked = widened * wide_live[:, None].astype(jnp.float32)
    totals = jnp.dot(
        inside.astype(jnp.float32),
        masked,
        precision=lax.Precision.HIGHEST,
        preferred_element_type=jnp.float32,
    )
    filtered = live_here * (traces * live_here - totals / divisor)
    spectra = spectrum(filtered, length_total)
    real_part = spectra[:, :FB]
    imag_part = spectra[:, FB:]
    power = (
        (real_part * real_part + imag_part * imag_part)
        .reshape(channels, FB // BAND, BAND)
        .mean(axis=2)
    )
    amplitude = jnp.repeat(jnp.sqrt(power + whiten_eps), BAND, axis=1)
    whitened = jnp.concatenate([real_part / amplitude, imag_part / amplitude], axis=1).astype(
        jnp.bfloat16
    )
    table = lag_weights(length_total)
    results = []
    moving = whitened
    for section in range(REACH):
        moving = shifted(moving, "fiber", -1)
        results.append(correlate_block(whitened, moving, table))
    return jnp.concatenate(results, axis=1)


def solution(mesh):
    return jax.shard_map(
        on_device,
        mesh=mesh,
        in_specs=(P("fiber", None), P("fiber"), P("fiber")),
        out_specs=P("fiber", None, None),
        check_vma=False,
    )
```

profile of v0, /device:TPU:32, one launch (start us, length us, event | category | flops | bytes accessed | tf_op | source)
XLA Modules:
  0.0 98.0 jit_solution(4078899028187076045)
XLA Ops:
  0.0 0.7 fusion.83
  0.8 1.9 %collective-permute-start = (s32[15]{0:T(128)S(1)}, s32[15]{0:T(128)S(1)}, u32[]{:S(2)}, u32[]{:S(2)}) collective-permute-start(s32[15]{0:T(128)S(1)} %get-tuple-element.413), channel_id=1, source_target_pairs={{0,1},{1,2},{2,3},{3,4},{4,5},{5,6},{6,7},{7,8},{8,9},{9,10},{10,1... | collective-permute-start | bytes 188 | tf_op jit(solution)/shard_map/ppermute | solution.py:26
  2.7 12.5 %collective-permute-start.1 = (s32[15]{0:T(128)S(1)}, s32[15]{0:T(128)S(1)}, u32[]{:S(2)}, u32[]{:S(2)}) collective-permute-start(s32[15]{0:T(128)S(1)} %get-tuple-element.414), channel_id=1, source_target_pairs={{1,0},{2,1},{3,2},{4,3},{5,4},{6,5},{7,6},{8,7},{9,8},{10,9},{11,1... | collective-permute-start | bytes 188 | tf_op jit(solution)/shard_map/ppermute | solution.py:29
  15.2 1.1 %fusion.82 = (f32[15,3000]{1,0:T(8,128)S(1)}, f32[15,3000]{1,0:T(8,128)S(1)}) fusion(f32[32,3000]{1,0:T(8,128)} %param.13), kind=kLoop, calls=%fused_computation.140 | loop fusion | bytes 720000 | tf_op jit(solution)/shard_map/slice | solution.py:27
  16.3 1.9 %collective-permute-start.2 = (f32[15,3000]{1,0:T(8,128)S(1)}, f32[15,3000]{1,0:T(8,128)S(1)}, u32[]{:S(2)}, u32[]{:S(2)}) collective-permute-start(f32[15,3000]{1,0:T(8,128)S(1)} %get-tuple-element.395), channel_id=1, source_target_pairs={{0,1},{1,2},{2,3},{3,4},{4,5},{5,6},{6,7},{7,8},{8,9},{9,10},{10,1... | collective-permute-start | bytes 540008 | tf_op jit(solution)/shard_map/ppermute | solution.py:26
  18.2 9.1 %collective-permute-start.3 = (f32[15,3000]{1,0:T(8,128)S(1)}, f32[15,3000]{1,0:T(8,128)S(1)}, u32[]{:S(2)}, u32[]{:S(2)}) collective-permute-start(f32[15,3000]{1,0:T(8,128)S(1)} %get-tuple-element.396), channel_id=1, source_target_pairs={{1,0},{2,1},{3,2},{4,3},{5,4},{6,5},{7,6},{8,7},{9,8},{10,9},{11,1... | collective-permute-start | bytes 540008 | tf_op jit(solution)/shard_map/ppermute | solution.py:29
  27.4 1.6 %fusion.65 = (f32[128,768]{1,0:T(8,128)S(1)}, f32[128,768]{1,0:T(8,128)S(1)}) fusion(s32[768]{0:T(1024)S(1)} %iota_add_fusion), kind=kLoop, calls=%fused_computation.95 | loop fusion | flops 983040 | bytes 789504 | tf_op jit(solution)/shard_map/cos | solution.py:60
  29.0 3.3 %fusion.59 = (f32[768,256]{1,0:T(8,128)S(1)}, f32[768,256]{1,0:T(8,128)S(1)}) fusion(s32[256]{0:T(256)S(1)} %iota_add_fusion.1, s32[768]{0:T(1024)S(1)} %iota_add_fusion), kind=kLoop, calls=%fused_computation.86 | loop fusion | flops 1966080 | bytes 1576960 | tf_op jit(solution)/shard_map/cos | solution.py:46
  33.3 0.6 fusion.49
  34.0 16.7 %while.62 = (s32[]{:T(128)}, f32[32,768]{1,0:T(8,128)S(1)}, f32[32,768]{1,0:T(8,128)S(1)}, f32[32,3072]{1,0:T(8,128)S(1)}, f32[128,1536]{1,0:T(8,128)S(1)}, /*index=5*/s32[]{:T(128)}, s32[]{:T(128)}, s32[]{:T(128)}, s32[]{:T(128)}) while((s32[]{:T(128)}, f32[32,768]{1,0:T(8,128)S(1)}, f32[32,768]{1,0:T(8,128)S(1)}, ...), condition=%wide.region_2.3_spmd.clone, body=%wide.region_1.2_spmd.clone.sunk | while | flops 75751688 | bytes 1601693 | solution.py:82
  34.0 0.5 fusion.121
  34.7 0.5 fusion.121
  35.4 0.5 fusion.121
  50.0 0.5 fusion.121
  51.2 6.3 %collective-permute-start.4 = (bf16[32,1536]{1,0:T(8,128)(2,1)S(1)}, bf16[32,1536]{1,0:T(8,128)(2,1)S(1)}, u32[]{:S(2)}, u32[]{:S(2)}) collective-permute-start(bf16[32,1536]{1,0:T(8,128)(2,1)S(1)} %pad_maximum_fusion.3), channel_id=1, source_target_pairs={{1,0},{2,1},{3,2},{4,3},{5,4},{6,5},{7,6},{8,7},{9,8},{10,9},{11,1... | collective-permute-start | bytes 294920 | tf_op jit(solution)/shard_map/ppermute | solution.py:37
  57.6 2.2 %collective-permute-done.4 = bf16[32,1536]{1,0:T(8,128)(2,1)S(1)} collective-permute-done((bf16[32,1536]{1,0:T(8,128)(2,1)S(1)}, bf16[32,1536]{1,0:T(8,128)(2,1)S(1)}, u32[]{:S(2)}, u32[]{:S(2)}) %collective-permute-start.4) | collective-permute-done | bytes 98336 | tf_op jit(solution)/shard_map/ppermute | solution.py:37
  59.8 9.2 %collective-permute-start.5 = (bf16[32,1536]{1,0:T(8,128)(2,1)S(1)}, bf16[32,1536]{1,0:T(8,128)(2,1)S(1)}, u32[]{:S(2)}, u32[]{:S(2)}) collective-permute-start(bf16[32,1536]{1,0:T(8,128)(2,1)S(1)} %collective-permute-done.4), channel_id=1, source_target_pairs={{1,0},{2,1},{3,2},{4,3},{5,4},{6,5},{7,6},{8,7},{9,8},{10,9},{11,1... | collective-permute-start | bytes 294920 | tf_op jit(solution)/shard_map/ppermute | solution.py:37
  69.0 2.3 %while.58 = (s32[]{:T(128)}, bf16[2,16,32,256]{3,2,1,0:T(8,128)(2,1)S(1)}, bf16[2,16,1536]{2,1,0:T(8,128)(2,1)S(1)}, f32[1,32,768]{2,1,0:T(8,128)S(1)}, f32[1,32...) while((s32[]{:T(128)}, bf16[2,16,32,256]{3,2,1,0:T(8,128)(2,1)S(1)}, ...), condition=%wide.region_5.6_spmd, body=%wide.region_4.5_spmd.sunk | while | flops 409100288 | bytes 5259349 | solution.py:104
  69.6 0.6 fusion.109
  70.7 0.6 fusion.109
  71.4 9.0 %collective-permute-start.6 = (bf16[32,1536]{1,0:T(8,128)(2,1)S(1)}, bf16[32,1536]{1,0:T(8,128)(2,1)S(1)}, u32[]{:S(2)}, u32[]{:S(2)}) collective-permute-start(bf16[32,1536]{1,0:T(8,128)(2,1)S(1)} %collective-permute-done.5), channel_id=1, source_target_pairs={{1,0},{2,1},{3,2},{4,3},{5,4},{6,5},{7,6},{8,7},{9,8},{10,9},{11,1... | collective-permute-start | bytes 294920 | tf_op jit(solution)/shard_map/ppermute | solution.py:37
  80.4 2.3 %while.59 = (s32[]{:T(128)}, bf16[2,16,32,256]{3,2,1,0:T(8,128)(2,1)S(1)}, bf16[2,16,1536]{2,1,0:T(8,128)(2,1)S(1)}, f32[1,32,768]{2,1,0:T(8,128)S(1)}, f32[1,32...) while((s32[]{:T(128)}, bf16[2,16,32,256]{3,2,1,0:T(8,128)(2,1)S(1)}, ...), condition=%wide.region_7.8_spmd, body=%wide.region_6.7_spmd.sunk | while | flops 409100288 | bytes 5259349 | solution.py:104
  81.0 0.6 fusion.112
  82.1 0.6 fusion.112
  82.7 9.0 %collective-permute-start.7 = (bf16[32,1536]{1,0:T(8,128)(2,1)S(1)}, bf16[32,1536]{1,0:T(8,128)(2,1)S(1)}, u32[]{:S(2)}, u32[]{:S(2)}) collective-permute-start(bf16[32,1536]{1,0:T(8,128)(2,1)S(1)} %collective-permute-done.6), channel_id=1, source_target_pairs={{1,0},{2,1},{3,2},{4,3},{5,4},{6,5},{7,6},{8,7},{9,8},{10,9},{11,1... | collective-permute-start | bytes 294920 | tf_op jit(solution)/shard_map/ppermute | solution.py:37
  91.8 2.3 %while.60 = (s32[]{:T(128)}, bf16[2,16,32,256]{3,2,1,0:T(8,128)(2,1)S(1)}, bf16[2,16,1536]{2,1,0:T(8,128)(2,1)S(1)}, f32[1,32,768]{2,1,0:T(8,128)S(1)}, f32[1,32...) while((s32[]{:T(128)}, bf16[2,16,32,256]{3,2,1,0:T(8,128)(2,1)S(1)}, ...), condition=%wide.region_9.10_spmd, body=%wide.region_8.9_spmd.sunk | while | flops 409100288 | bytes 5259349 | solution.py:104
  92.3 0.6 fusion.115
  93.5 0.6 fusion.115
  94.2 2.3 %while.61 = (s32[]{:T(128)}, bf16[2,16,32,256]{3,2,1,0:T(8,128)(2,1)S(1)}, bf16[2,16,1536]{2,1,0:T(8,128)(2,1)S(1)}, f32[1,32,768]{2,1,0:T(8,128)S(1)}, f32[1,32...) while((s32[]{:T(128)}, bf16[2,16,32,256]{3,2,1,0:T(8,128)(2,1)S(1)}, ...), condition=%wide.region_11.12_spmd, body=%wide.region_10.11_spmd.sunk | while | flops 409100288 | bytes 5259349 | solution.py:104
  94.7 0.6 fusion.118
  95.9 0.6 fusion.118
  96.5 1.5 %pad_maximum_fusion = bf16[32,128,256]{2,1,0:T(8,128)(2,1)} fusion(bf16[32,32,256]{2,1,0:T(8,128)(2,1)S(1)} %bitcast.157, bf16[32,32,256]{2,1,0:T(8,128)(2,1)S(1)} %bitcast.160, bf16[32,32,256]{2,1,0:T(8,128)(2,1)S(1)} %bitcast.159, bf16[32,32,256]{2,1,0:T(8,128)(2,1)S(1)} %bitcast.158), kind=kLoop, calls=%fused_computation.70 | loop fusion | flops 8388608 | bytes 4194304 | tf_op jit(solution)/shard_map/concatenate | solution.py:151
  (143 shorter events, 19.8 us)
Async XLA Ops:
  0.8 31.7 %collective-permute-start = (s32[15]{0:T(128)S(1)}, s32[15]{0:T(128)S(1)}, u32[]{:S(2)}, u32[]{:S(2)}) collective-permute-start(s32[15]{0:T(128)S(1)} %get-tuple-element.413), channel_id=1, source_target_pairs={{0,1},{1,2},{2,3},{3,4},{4,5},{5,6},{6,7},{7,8},{8,9},{9,10},{10,1... | collective-permute-start | bytes 188 | tf_op jit(solution)/shard_map/ppermute | solution.py:26
  2.7 29.8 %collective-permute-start.1 = (s32[15]{0:T(128)S(1)}, s32[15]{0:T(128)S(1)}, u32[]{:S(2)}, u32[]{:S(2)}) collective-permute-start(s32[15]{0:T(128)S(1)} %get-tuple-element.414), channel_id=1, source_target_pairs={{1,0},{2,1},{3,2},{4,3},{5,4},{6,5},{7,6},{8,7},{9,8},{10,9},{11,1... | collective-permute-start | bytes 188 | tf_op jit(solution)/shard_map/ppermute | solution.py:29
  16.3 16.9 %collective-permute-start.2 = (f32[15,3000]{1,0:T(8,128)S(1)}, f32[15,3000]{1,0:T(8,128)S(1)}, u32[]{:S(2)}, u32[]{:S(2)}) collective-permute-start(f32[15,3000]{1,0:T(8,128)S(1)} %get-tuple-element.395), channel_id=1, source_target_pairs={{0,1},{1,2},{2,3},{3,4},{4,5},{5,6},{6,7},{7,8},{8,9},{9,10},{10,1... | collective-permute-start | bytes 540008 | tf_op jit(solution)/shard_map/ppermute | solution.py:26
  18.2 15.0 %collective-permute-start.3 = (f32[15,3000]{1,0:T(8,128)S(1)}, f32[15,3000]{1,0:T(8,128)S(1)}, u32[]{:S(2)}, u32[]{:S(2)}) collective-permute-start(f32[15,3000]{1,0:T(8,128)S(1)} %get-tuple-element.396), channel_id=1, source_target_pairs={{1,0},{2,1},{3,2},{4,3},{5,4},{6,5},{7,6},{8,7},{9,8},{10,9},{11,1... | collective-permute-start | bytes 540008 | tf_op jit(solution)/shard_map/ppermute | solution.py:29
  32.3 0.7 copy-start.1
  32.3 1.0 %copy-start = (f32[32,3000]{1,0:T(8,128)S(1)}, f32[32,3000]{1,0:T(8,128)}, u32[]{:S(2)}) copy-start(f32[32,3000]{1,0:T(8,128)} %param.13) | copy-start | bytes 1152004
  51.2 8.5 %collective-permute-start.4 = (bf16[32,1536]{1,0:T(8,128)(2,1)S(1)}, bf16[32,1536]{1,0:T(8,128)(2,1)S(1)}, u32[]{:S(2)}, u32[]{:S(2)}) collective-permute-start(bf16[32,1536]{1,0:T(8,128)(2,1)S(1)} %pad_maximum_fusion.3), channel_id=1, source_target_pairs={{1,0},{2,1},{3,2},{4,3},{5,4},{6,5},{7,6},{8,7},{9,8},{10,9},{11,1... | collective-permute-start | bytes 294920 | tf_op jit(solution)/shard_map/ppermute | solution.py:37
  59.8 11.5 %collective-permute-start.5 = (bf16[32,1536]{1,0:T(8,128)(2,1)S(1)}, bf16[32,1536]{1,0:T(8,128)(2,1)S(1)}, u32[]{:S(2)}, u32[]{:S(2)}) collective-permute-start(bf16[32,1536]{1,0:T(8,128)(2,1)S(1)} %collective-permute-done.4), channel_id=1, source_target_pairs={{1,0},{2,1},{3,2},{4,3},{5,4},{6,5},{7,6},{8,7},{9,8},{10,9},{11,1... | collective-permute-start | bytes 294920 | tf_op jit(solution)/shard_map/ppermute | solution.py:37
  71.4 11.3 %collective-permute-start.6 = (bf16[32,1536]{1,0:T(8,128)(2,1)S(1)}, bf16[32,1536]{1,0:T(8,128)(2,1)S(1)}, u32[]{:S(2)}, u32[]{:S(2)}) collective-permute-start(bf16[32,1536]{1,0:T(8,128)(2,1)S(1)} %collective-permute-done.5), channel_id=1, source_target_pairs={{1,0},{2,1},{3,2},{4,3},{5,4},{6,5},{7,6},{8,7},{9,8},{10,9},{11,1... | collective-permute-start | bytes 294920 | tf_op jit(solution)/shard_map/ppermute | solution.py:37
  82.7 11.4 %collective-permute-start.7 = (bf16[32,1536]{1,0:T(8,128)(2,1)S(1)}, bf16[32,1536]{1,0:T(8,128)(2,1)S(1)}, u32[]{:S(2)}, u32[]{:S(2)}) collective-permute-start(bf16[32,1536]{1,0:T(8,128)(2,1)S(1)} %collective-permute-done.6), channel_id=1, source_target_pairs={{1,0},{2,1},{3,2},{4,3},{5,4},{6,5},{7,6},{8,7},{9,8},{10,9},{11,1... | collective-permute-start | bytes 294920 | tf_op jit(solution)/shard_map/ppermute | solution.py:37
where the time goes:
time: 98.3 us; the launch traced here: 98 us
  starting transfers between devices  58.9 us (60%)
  matrix products  17.8 us (18%)
  other arithmetic  15 us (15%)
  local copies, waits for them, and re-layouts  2.44 us (2%)
  waiting for transfers between devices  2.19 us (2%)
  loops' own time  1.29 us (1%)
    ppermute x4, starting transfers between devices, shifted(): lax.ppermute(value, axis, [(source, source + steps) for source in range(l...  33.5 us
    ppermute x2, starting transfers between devices, with_halo(): lax.ppermute(lax.slice_in_dim(block, 0, width, axis=dim), axis, backward)  21.5 us
    dot_general x24, matrix products, add_span(): jnp.dot(window, base, precision=lax.Precision.HIGHEST, preferred_element_...  12.6 us
    dot_general x8, matrix products, one_group(): result = jnp.dot(cross, table, preferred_element_type=jnp.float32)  4.57 us
    ppermute x2, starting transfers between devices, with_halo(): lax.ppermute(lax.slice_in_dim(block, block.shape[dim] - width, None, axis...  3.83 us
    convert_element_type x8, other arithmetic, one_group(): (own_real * partner_real + own_imag * partner_imag).astype(jnp.bfloat16)  3.78 us
    cos x1, other arithmetic, lag_weights(): jnp.cos(phases)  3.26 us
    ppermute x4, waiting for transfers between devices, shifted(): lax.ppermute(value, axis, [(source, source + steps) for source in range(l...  2.18 us
  transfers between devices with their start and end apart: 8, of which 1 were waited for; matrix products, arithmetic and copies ran while one was open for 13% of the time, Pallas kernels for 0%

commit v1 on v0

v1 whole, which is shorter than its diff:
```python
import functools
import math

import jax
import jax.numpy as jnp
import ml_dtypes
import numpy as np
from jax import lax
from jax.experimental import pallas as pl
from jax.experimental.pallas import tpu as pltpu
from jax.sharding import PartitionSpec as P

LOW_BIN = 32
FB = 768
BAND = 64
HALF_WIN = 15
LAGS = 256
CH = 32
HALF = 16
REACH = 4
SPAN = 256
CHUNK = 256
WHITEN_EPS = 1.0
MESH = pl.DeviceIdType.MESH


def tables(length):
    bins = LOW_BIN + np.arange(FB)
    taper = np.sin(np.pi * (np.arange(FB) + 0.5) / FB)
    angle = 2.0 * np.pi / length * np.mod(np.arange(SPAN)[:, None] * bins[None, :], length)
    base = np.concatenate([np.cos(angle) * taper, -np.sin(angle) * taper], axis=1)
    high = base.astype(ml_dtypes.bfloat16)
    low = (base - high.astype(np.float64)).astype(ml_dtypes.bfloat16)
    turn = 2.0 * np.pi / length * np.mod(SPAN * bins, length)
    twiddle = np.stack([np.cos(turn), -np.sin(turn)]).astype(np.float32)
    band = np.arange(CHUNK) // BAND
    same = (band[:, None] == band[None, :]).astype(ml_dtypes.bfloat16)
    lag = np.arange(LAGS) - LAGS // 2
    phase = 2.0 * np.pi / length * np.mod(bins[:, None] * lag[None, :], length)
    lags = np.concatenate([np.cos(phase), -np.sin(phase)], axis=0) / math.sqrt(FB)
    return high, low, twiddle, same, lags.astype(np.float32).astype(ml_dtypes.bfloat16)


def split3(value):
    first = value.astype(jnp.bfloat16)
    rest = value - first.astype(jnp.float32)
    second = rest.astype(jnp.bfloat16)
    third = (rest - second.astype(jnp.float32)).astype(jnp.bfloat16)
    return first, second, third


def dot(a, b):
    return jnp.dot(a, b, preferred_element_type=jnp.float32)


def spectra_kernel(
    count,
    traces_hbm, live_ref, segment_ref, high_hbm, low_hbm, twiddle_ref, same_ref,
    rows_ref,
    traces, high, low, first, second, spec, labels, whole,
    in_sem, here_sem, halo_send, halo_recv, row_send, row_recv,
):
    me = lax.axis_index("fiber")
    core = lax.rem(me, 2)
    depth = lax.rem(me // 2, 8)
    length = traces.shape[1]
    spans = -(-length // SPAN)

    loads = [
        pltpu.make_async_copy(traces_hbm, traces, in_sem.at[0]),
        pltpu.make_async_copy(high_hbm, high, in_sem.at[1]),
        pltpu.make_async_copy(low_hbm, low, in_sem.at[2]),
    ]
    for load in loads:
        load.start()

    barrier = pltpu.get_barrier_semaphore()

    def exists(step):
        return (me + step >= 0) & (me + step < count)

    def on(condition, action):
        pl.when(condition)(action)

    for step in (1, 2, 4):
        on(
            exists(-step),
            lambda: pl.semaphore_signal(barrier, inc=1, device_id=(me - step,), device_id_type=MESH),
        )

    def greet():
        peers = sum(jnp.where(exists(step), 1, 0) for step in (1, 2, 4))
        on(exists(1), lambda: pl.semaphore_wait(barrier, peers))
        for slot, step in enumerate((1, 2, 4)):
            on(
                exists(step),
                lambda: pl.semaphore_signal(
                    here_sem.at[slot], inc=1, device_id=(me + step,), device_id_type=MESH
                ),
            )

    whole[...] = jnp.zeros_like(whole)
    whole[0:1, 0:CH] = segment_ref[...] * 2 + live_ref[...]
    packed = whole[...]
    lane = lax.broadcasted_iota(jnp.int32, (8, 128), 1)
    own_labels = pltpu.roll(packed, HALF, 1)
    labels[0] = own_labels
    labels[1] = jnp.where(lane < HALF, pltpu.roll(packed, 128 - HALF, 1), 0)
    labels[2] = jnp.where((lane >= CH + HALF) & (lane < CH + 2 * HALF), pltpu.roll(packed, CH + HALF, 1), 0)

    last = depth == 7
    on(last, greet)

    loads[0].wait()
    for s in range(spans):
        piece = traces[:, s * SPAN : min(length, (s + 1) * SPAN)]
        if piece.shape[1] < SPAN:
            piece = jnp.concatenate([piece, jnp.zeros((CH, SPAN - piece.shape[1]), jnp.float32)], axis=1)
        top = piece.astype(jnp.bfloat16)
        first[s * CH : (s + 1) * CH, :] = top
        second[s * CH : (s + 1) * CH, :] = (piece - top.astype(jnp.float32)).astype(jnp.bfloat16)
    loads[1].wait()
    loads[2].wait()
    for c in range(FB // CHUNK):
        parts = []
        for offset in (c * CHUNK, FB + c * CHUNK):
            cols = slice(offset, offset + CHUNK)
            parts.append(
                dot(first[...], high[:, cols]) + dot(second[...], high[:, cols]) + dot(first[...], low[:, cols])
            )
        cosine = twiddle_ref[0:1, c * CHUNK : (c + 1) * CHUNK]
        sine = twiddle_ref[1:2, c * CHUNK : (c + 1) * CHUNK]
        real = parts[0][(spans - 1) * CH :, :]
        imag = parts[1][(spans - 1) * CH :, :]
        for s in range(spans - 2, -1, -1):
            rows = slice(s * CH, (s + 1) * CH)
            real, imag = (
                parts[0][rows, :] + (real * cosine - imag * sine),
                parts[1][rows, :] + (real * sine + imag * cosine),
            )
        spec[HALF : HALF + CH, c * CHUNK : (c + 1) * CHUNK] = real
        spec[HALF : HALF + CH, FB + c * CHUNK : FB + (c + 1) * CHUNK] = imag

    on(jnp.logical_not(last), greet)

    def remote(src, dst, send, recv, target):
        return pltpu.make_async_remote_copy(
            src_ref=src, dst_ref=dst, send_sem=send, recv_sem=recv, device_id=(target,), device_id_type=MESH
        )

    right = [
        remote(spec.at[pl.ds(CH, HALF)], spec.at[pl.ds(0, HALF)], halo_send.at[0], halo_recv.at[0], me + 1),
        remote(labels.at[1], labels.at[3], halo_send.at[1], halo_recv.at[1], me + 1),
    ]
    left = [
        remote(spec.at[pl.ds(HALF, HALF)], spec.at[pl.ds(CH + HALF, HALF)], halo_send.at[2], halo_recv.at[2], me - 1),
        remote(labels.at[2], labels.at[4], halo_send.at[3], halo_recv.at[3], me - 1),
    ]

    def start_all(copies):
        for copy in copies:
            copy.start()

    on(exists(1), lambda: start_all(right))

    def send_left():
        pl.semaphore_wait(here_sem.at[0], 1)
        start_all(left)

    late = (depth == 0) & (core == 0)
    on(exists(-1) & jnp.logical_not(late), send_left)

    def row_slice(block, half):
        return rows_ref.at[pl.ds(block * CH + half * HALF, HALF)]

    def row_copy(kind, half, source, target_block, target):
        return remote(
            row_slice(source, half), row_slice(target_block, half),
            row_send.at[kind, half], row_recv.at[target_block - 1, half], target,
        )

    def own_copies(half):
        return [
            (row_copy(0, half, 0, 1, me - 1), core == 1),
            (row_copy(1, half, 0, 2, me - 2), exists(-2)),
            (row_copy(2, half, 0, 4, me - 4), exists(-4)),
        ]

    wide_row = lax.broadcasted_iota(jnp.int32, (CH, 128), 0) + HALF
    wide_lane = lax.broadcasted_iota(jnp.int32, (CH, 128), 1)
    near = jnp.abs(wide_lane - wide_row) <= HALF_WIN

    def whiten(half, received):
        base = half * HALF
        mine = jnp.where(wide_lane == wide_row, labels[0, 0:1, :], 0).astype(jnp.float32)
        mine = jnp.sum(mine, axis=1, keepdims=True).astype(jnp.int32)
        wide = labels[0, 0:1, :] + received
        keep = near & ((wide >> 1) == (mine >> 1)) & ((wide & 1) == 1)
        inside = jnp.where(keep, 1.0, 0.0)
        divisor = jnp.maximum(jnp.sum(inside, axis=1, keepdims=True), 1.0)[base : base + HALF]
        alive = (mine & 1).astype(jnp.float32)[base : base + HALF]
        weights = inside[base : base + HALF, base : base + 3 * HALF].astype(jnp.bfloat16)
        weights = jnp.concatenate([weights, weights, weights], axis=1)
        for c in range(FB // CHUNK):
            parts = []
            for offset in (c * CHUNK, FB + c * CHUNK):
                cols = slice(offset, offset + CHUNK)
                stack = jnp.concatenate(split3(spec[base : base + 3 * HALF, cols]), axis=0)
                total = dot(weights, stack)
                value = spec[HALF + base : 2 * HALF + base, cols]
                parts.append(alive * (value * alive - total / divisor))
            square = parts[0] * parts[0] + parts[1] * parts[1]
            sums = dot(jnp.concatenate(split3(square), axis=0), same_ref[...])
            power = (sums[:HALF] + (sums[HALF : 2 * HALF] + sums[2 * HALF :])) * (1.0 / BAND)
            scale = lax.rsqrt(power + WHITEN_EPS)
            rows_ref[base : base + HALF, c * CHUNK : (c + 1) * CHUNK] = (parts[0] * scale).astype(jnp.bfloat16)
            rows_ref[base : base + HALF, FB + c * CHUNK : FB + (c + 1) * CHUNK] = (parts[1] * scale).astype(jnp.bfloat16)

    def receive(copies):
        for copy in copies:
            copy.wait_recv()

    def blank(ref_rows):
        rows_ref[ref_rows, :] = jnp.zeros((CH, 2 * FB), jnp.bfloat16)

    for block in range(1, REACH + 1):
        on(jnp.logical_not(exists(block)), functools.partial(blank, slice(block * CH, (block + 1) * CH)))

    def no_right():
        spec[CH + HALF :, :] = jnp.zeros((HALF, 2 * FB), jnp.float32)
        labels[4] = jnp.zeros((8, 128), jnp.int32)

    def no_left():
        spec[0:HALF, :] = jnp.zeros((HALF, 2 * FB), jnp.float32)
        labels[3] = jnp.zeros((8, 128), jnp.int32)

    on(exists(1), lambda: receive(left))
    on(jnp.logical_not(exists(1)), no_right)
    whiten(1, labels[4, 0:1, :])
    on(exists(-1) & late, send_left)
    on(core == 1, own_copies(1)[0][0].start)

    def meet(slot):
        pl.semaphore_wait(here_sem.at[slot], 1)

    on(exists(-2), lambda: meet(1))
    on(exists(-2), own_copies(1)[1][0].start)
    on(exists(-4), lambda: meet(2))
    on(exists(-4), own_copies(1)[2][0].start)

    on(exists(-1), lambda: receive(right))
    on(jnp.logical_not(exists(-1)), no_left)
    whiten(0, labels[3, 0:1, :])
    for copy, condition in own_copies(0):
        on(condition, copy.start)

    def arrived(block, half):
        row_copy(0, half, 0, block, me).wait_recv()

    passed = []
    for half in (1, 0):
        on(exists(2), functools.partial(arrived, 2, half))
        to_high = row_copy(3, half, 2, 1, me + 1)
        to_low = row_copy(3, half, 2, 3, me - 1)
        on(exists(2) & (core == 0), to_high.start)
        on(exists(2) & (core == 1), to_low.start)
        passed += [(to_high, exists(2))]
    for half in (1, 0):
        on(exists(4), functools.partial(arrived, 4, half))
        to_high = row_copy(4, half, 4, 3, me + 1)
        on(exists(4) & (core == 0), to_high.start)
        passed += [(to_high, exists(4) & (core == 0))]
    for block in (1, 3):
        for half in (1, 0):
            on(exists(block), functools.partial(arrived, block, half))

    def sent(copies):
        for copy in copies:
            copy.wait_send()

    on(exists(1), lambda: sent(right))
    on(exists(-1), lambda: sent(left))
    for half in (1, 0):
        for copy, condition in own_copies(half):
            on(condition, copy.wait_send)
    for copy, condition in passed:
        on(condition, copy.wait_send)


GROUP = 8


def correlate_kernel(rows_ref, table_ref, out_ref):
    group = pl.program_id(0)
    own = rows_ref[pl.ds(pl.multiple_of(lax.div(group, 2) * HALF, HALF), HALF), :].astype(jnp.float32)
    own = jnp.where(lax.rem(group, 2) == 0, own[:GROUP], own[GROUP:])
    total = None
    for c in range(FB // CHUNK):
        re_cols = slice(c * CHUNK, (c + 1) * CHUNK)
        im_cols = slice(FB + c * CHUNK, FB + (c + 1) * CHUNK)
        own_re = own[:, None, re_cols]
        own_im = own[:, None, im_cols]
        far_re = rows_ref[CH:, re_cols].astype(jnp.float32)[None]
        far_im = rows_ref[CH:, im_cols].astype(jnp.float32)[None]
        real = (own_re * far_re + own_im * far_im).astype(jnp.bfloat16).reshape(GROUP * REACH * CH, CHUNK)
        imag = (own_im * far_re - own_re * far_im).astype(jnp.bfloat16).reshape(GROUP * REACH * CH, CHUNK)
        term = dot(real, table_ref[re_cols, :]) + dot(imag, table_ref[im_cols, :])
        total = term if total is None else total + term
    out_ref[...] = total.astype(jnp.bfloat16).reshape(GROUP, REACH * CH, LAGS)


def on_device(traces, live, segment):
    count = lax.axis_size("fiber")
    channels, length = traces.shape
    high, low, twiddle, same, lags = (jnp.asarray(t) for t in tables(length))
    anywhere = pl.BlockSpec(memory_space=pl.ANY)
    in_vmem = pl.BlockSpec(memory_space=pltpu.VMEM)
    spans = -(-length // SPAN)
    rows = pl.pallas_call(
        functools.partial(spectra_kernel, count),
        out_shape=jax.ShapeDtypeStruct(((1 + REACH) * channels, 2 * FB), jnp.bfloat16),
        in_specs=[anywhere, in_vmem, in_vmem, anywhere, anywhere, in_vmem, in_vmem],
        out_specs=in_vmem,
        scratch_shapes=[
            pltpu.VMEM((channels, length), jnp.float32),
            pltpu.VMEM((SPAN, 2 * FB), jnp.bfloat16),
            pltpu.VMEM((SPAN, 2 * FB), jnp.bfloat16),
            pltpu.VMEM((spans * CH, SPAN), jnp.bfloat16),
            pltpu.VMEM((spans * CH, SPAN), jnp.bfloat16),
            pltpu.VMEM((2 * CH, 2 * FB), jnp.float32),
            pltpu.VMEM((5, 8, 128), jnp.int32),
            pltpu.VMEM((8, 128), jnp.int32),
            pltpu.SemaphoreType.DMA((3,)),
            pltpu.SemaphoreType.REGULAR((3,)),
            pltpu.SemaphoreType.DMA((4,)),
            pltpu.SemaphoreType.DMA((4,)),
            pltpu.SemaphoreType.DMA((5, 2)),
            pltpu.SemaphoreType.DMA((4, 2)),
        ],
        compiler_params=pltpu.CompilerParams(
            collective_id=0, has_side_effects=True, vmem_limit_bytes=40 * 1024 * 1024
        ),
        name="spectra",
    )(traces, live.reshape(1, channels), segment.reshape(1, channels), high, low, twiddle, same)
    return pl.pallas_call(
        correlate_kernel,
        grid=(channels // GROUP,),
        out_shape=jax.ShapeDtypeStruct((channels, REACH * channels, LAGS), jnp.bfloat16),
        in_specs=[
            pl.BlockSpec(((1 + REACH) * channels, 2 * FB), lambda g: (0, 0)),
            pl.BlockSpec((2 * FB, LAGS), lambda g: (0, 0)),
        ],
        out_specs=pl.BlockSpec((GROUP, REACH * channels, LAGS), lambda g: (g, 0, 0)),
        compiler_params=pltpu.CompilerParams(vmem_limit_bytes=48 * 1024 * 1024),
        name="correlate",
    )(rows, lags)


def solution(mesh):
    return jax.shard_map(
        on_device,
        mesh=mesh,
        in_specs=(P("fiber", None), P("fiber"), P("fiber")),
        out_specs=P("fiber", None, None),
        check_vma=False,
    )
```

time: 98.3 us -> 33.6 us (0.34)
  the two profiles are of different devices: /device:TPU:32 before, /device:TPU:17 now
where the time goes in v1:
time: 33.6 us; the launch traced here: 33.3 us
  Pallas kernels  27.1 us (81%)
  local copies, waits for them, and re-layouts  6.24 us (19%)
    pallas_call x1, Pallas kernels, on_device(): pl.pallas_call(functools.partial(spectra_kernel, count), out_shape=jax.Sh...  22.2 us
    unnamed x16, local copies, waits for them, and re-layouts  6.24 us
    pallas_call x1, Pallas kernels, on_device(): pl.pallas_call(correlate_kernel, grid=(channels // GROUP,), out_shape=jax...  4.89 us

profile of v1, /device:TPU:17, one launch (start us, length us, event | category | flops | bytes accessed | tf_op | source)
XLA Modules:
  0.0 33.3 jit_solution(15608556827900840044)
XLA Ops:
  0.0 0.0 copy-start
  0.0 0.0 copy-start.1
  0.0 1.2 %copy-done.1 = bf16[256,1536]{1,0:T(8,128)(2,1)S(1)} copy-done((bf16[256,1536]{1,0:T(8,128)(2,1)S(1)}, bf16[256,1536]{1,0:T(8,128)(2,1)}, u32[]{:S(2)}) %copy-start.1) | copy-done | bytes 786456
  1.2 0.0 copy-start.2
  1.2 1.1 %copy-done.2 = bf16[256,1536]{1,0:T(8,128)(2,1)S(1)} copy-done((bf16[256,1536]{1,0:T(8,128)(2,1)S(1)}, bf16[256,1536]{1,0:T(8,128)(2,1)}, u32[]{:S(2)}) %copy-start.2) | copy-done | bytes 786456
  2.3 0.0 copy-start.3
  2.3 1.0 %copy-done.3 = f32[32,3000]{1,0:T(8,128)S(1)} copy-done((f32[32,3000]{1,0:T(8,128)S(1)}, f32[32,3000]{1,0:T(8,128)}, u32[]{:S(2)}) %copy-start.3) | copy-done | bytes 384024
  3.3 0.0 copy-start.4
  3.3 0.9 %copy-done.4 = bf16[256,256]{1,0:T(8,128)(2,1)S(1)} copy-done((bf16[256,256]{1,0:T(8,128)(2,1)S(1)}, bf16[256,256]{1,0:T(8,128)(2,1)}, u32[]{:S(2)}) %copy-start.4) | copy-done | bytes 131096
  4.2 0.0 copy-start.5
  4.2 0.7 %copy-done.5 = f32[2,768]{1,0:T(2,128)S(1)} copy-done((f32[2,768]{1,0:T(2,128)S(1)}, f32[2,768]{1,0:T(2,128)}, u32[]{:S(2)}) %copy-start.5) | copy-done | bytes 6168
  4.9 0.0 copy-start.6
  4.9 0.7 %copy-done.6 = s32[32]{0:T(128)S(1)} copy-done((s32[32]{0:T(128)S(1)}, s32[32]{0:T(128)}, u32[]{:S(2)}) %copy-start.6) | copy-done | bytes 152
  5.6 0.0 copy-start.7
  5.6 0.7 %copy-done.7 = s32[32]{0:T(128)S(1)} copy-done((s32[32]{0:T(128)S(1)}, s32[32]{0:T(128)}, u32[]{:S(2)}) %copy-start.7) | copy-done | bytes 152
  6.2 22.2 %spectra.1.rows_ref = bf16[160,1536]{1,0:T(8,128)(2,1)S(1)} custom-call(f32[32,3000]{1,0:T(8,128)S(1)} %copy-done.3, s32[1,32]{1,0:T(1,128)S(1)} %bitcast.2, s32[1,32]{1,0:T(1,128)S(1)} %bitcast.3, bf16[256,1536]{1,0:T(8,128)(2,1)S(1)} %copy-done.2, bf16[256,1536]{1,0:T(8,128)(2,1)S(1)} %copy-done.1, f32[2,768]{1,0:T(2,128)S(1)} %copy-done.5, ...), custom_call_target="tpu_custom_call" | custom-call | tf_op jit(solution)/shard_map/spectra/pallas_call | solution.py:319
  28.4 0.0 copy-done
  28.4 4.9 %correlate.1 = bf16[32,128,256]{2,1,0:T(8,128)(2,1)} custom-call(bf16[160,1536]{1,0:T(8,128)(2,1)S(1)} %spectra.1.rows_ref, bf16[1536,256]{1,0:T(8,128)(2,1)S(1)} %copy-done), custom_call_target="tpu_custom_call" | custom-call | tf_op jit(solution)/shard_map/correlate/pallas_call | solution.py:345
Async XLA Ops:
  0.0 28.4 %copy-start = (bf16[1536,256]{1,0:T(8,128)(2,1)S(1)}, bf16[1536,256]{1,0:T(8,128)(2,1)}, u32[]{:S(2)}) copy-start(bf16[1536,256]{1,0:T(8,128)(2,1)} %constant.14.clone.table_ref) | copy-start | bytes 2359300
  0.0 1.2 %copy-start.1 = (bf16[256,1536]{1,0:T(8,128)(2,1)S(1)}, bf16[256,1536]{1,0:T(8,128)(2,1)}, u32[]{:S(2)}) copy-start(bf16[256,1536]{1,0:T(8,128)(2,1)} %constant.11.clone.low_hbm) | copy-start | bytes 2359300
  1.2 1.1 %copy-start.2 = (bf16[256,1536]{1,0:T(8,128)(2,1)S(1)}, bf16[256,1536]{1,0:T(8,128)(2,1)}, u32[]{:S(2)}) copy-start(bf16[256,1536]{1,0:T(8,128)(2,1)} %constant.10.clone.high_hbm) | copy-start | bytes 2359300
  2.3 1.0 %copy-start.3 = (f32[32,3000]{1,0:T(8,128)S(1)}, f32[32,3000]{1,0:T(8,128)}, u32[]{:S(2)}) copy-start(f32[32,3000]{1,0:T(8,128)} %traces_hbm.1) | copy-start | bytes 1152004
  3.3 0.9 %copy-start.4 = (bf16[256,256]{1,0:T(8,128)(2,1)S(1)}, bf16[256,256]{1,0:T(8,128)(2,1)}, u32[]{:S(2)}) copy-start(bf16[256,256]{1,0:T(8,128)(2,1)} %constant.13.clone.same_ref) | copy-start | bytes 393220
  4.2 0.7 %copy-start.5 = (f32[2,768]{1,0:T(2,128)S(1)}, f32[2,768]{1,0:T(2,128)}, u32[]{:S(2)}) copy-start(f32[2,768]{1,0:T(2,128)} %constant.12.clone.twiddle_ref) | copy-start | bytes 18436
  4.9 0.7 %copy-start.6 = (s32[32]{0:T(128)S(1)}, s32[32]{0:T(128)}, u32[]{:S(2)}) copy-start(s32[32]{0:T(128)} %param.9) | copy-start | bytes 388
  5.6 0.7 %copy-start.7 = (s32[32]{0:T(128)S(1)}, s32[32]{0:T(128)}, u32[]{:S(2)}) copy-start(s32[32]{0:T(128)} %param.10) | copy-start | bytes 388

commit v2 on v1

v2 whole, which is shorter than its diff:
```python
import functools
import math

import jax
import jax.numpy as jnp
import ml_dtypes
import numpy as np
from jax import lax
from jax.experimental import pallas as pl
from jax.experimental.pallas import tpu as pltpu
from jax.sharding import PartitionSpec as P

LOW_BIN = 32
FB = 768
BAND = 64
HALF_WIN = 15
LAGS = 256
CH = 32
HALF = 16
REACH = 4
SPAN = 256
CHUNK = 256
WHITEN_EPS = 1.0
MESH = pl.DeviceIdType.MESH


CHUNKS = FB // CHUNK
WIDE = 2 * CHUNK


def chunk_major(table, axis):
    halves = np.split(table, 2, axis=axis)
    pieces = [np.split(half, CHUNKS, axis=axis) for half in halves]
    return [np.concatenate([pieces[0][c], pieces[1][c]], axis=axis) for c in range(CHUNKS)]


def tables(length):
    bins = LOW_BIN + np.arange(FB)
    taper = np.sin(np.pi * (np.arange(FB) + 0.5) / FB)
    angle = 2.0 * np.pi / length * np.mod(np.arange(SPAN)[:, None] * bins[None, :], length)
    base = np.concatenate([np.cos(angle) * taper, -np.sin(angle) * taper], axis=1)
    base = np.stack(chunk_major(base, 1))
    high = base.astype(ml_dtypes.bfloat16)
    low = (base - high.astype(np.float64)).astype(ml_dtypes.bfloat16)
    turn = 2.0 * np.pi / length * np.mod(SPAN * bins, length)
    twiddle = np.stack([np.cos(turn), -np.sin(turn)]).astype(np.float32)
    lag = np.arange(LAGS) - LAGS // 2
    phase = 2.0 * np.pi / length * np.mod(bins[:, None] * lag[None, :], length)
    lags = np.concatenate([np.cos(phase), -np.sin(phase)], axis=0) / math.sqrt(FB)
    lags = np.concatenate(chunk_major(lags.astype(np.float32), 0), axis=0)
    return np.stack([high, low], axis=1), twiddle, lags.astype(ml_dtypes.bfloat16)


def split3(value):
    first = value.astype(jnp.bfloat16)
    rest = value - first.astype(jnp.float32)
    second = rest.astype(jnp.bfloat16)
    third = (rest - second.astype(jnp.float32)).astype(jnp.bfloat16)
    return first, second, third


def dot(a, b):
    return jnp.dot(a, b, preferred_element_type=jnp.float32)


def correlate(own, far, table_ref):
    total = None
    for c in range(CHUNKS):
        re_cols = slice(c * WIDE, c * WIDE + CHUNK)
        im_cols = slice(c * WIDE + CHUNK, (c + 1) * WIDE)
        own_re = own[:, None, re_cols]
        own_im = own[:, None, im_cols]
        far_re = far(re_cols).astype(jnp.float32)[None]
        far_im = far(im_cols).astype(jnp.float32)[None]
        shape = (own.shape[0] * far_re.shape[1], CHUNK)
        real = (own_re * far_re + own_im * far_im).astype(jnp.bfloat16).reshape(shape)
        imag = (own_im * far_re - own_re * far_im).astype(jnp.bfloat16).reshape(shape)
        term = dot(real, table_ref[re_cols, :]) + dot(imag, table_ref[im_cols, :])
        total = term if total is None else total + term
    return total.astype(jnp.bfloat16).reshape(own.shape[0], -1, LAGS)


def spectra_kernel(
    count,
    traces_hbm, live_hbm, segment_hbm, base_hbm, twiddle_hbm, table_hbm,
    rows_ref, part_ref,
    traces, live, segment, base, twiddle, table, first, second, spec, labels, whole,
    in_sem, here_sem, halo_send, halo_recv, row_send, row_recv,
):
    me = lax.axis_index("fiber")
    core = lax.rem(me, 2)
    depth = lax.rem(me // 2, 8)
    length = traces.shape[1]
    spans = -(-length // SPAN)

    barrier = pltpu.get_barrier_semaphore()

    def exists(step):
        return (me + step >= 0) & (me + step < count)

    def on(condition, action):
        pl.when(condition)(action)

    def signal(semaphore, step):
        pl.semaphore_signal(semaphore, inc=1, device_id=(me + step,), device_id_type=MESH)

    for step in (1, 2):
        on(exists(-step), functools.partial(signal, barrier, -step))

    small = [
        pltpu.make_async_copy(live_hbm, live, in_sem.at[0]),
        pltpu.make_async_copy(segment_hbm, segment, in_sem.at[1]),
        pltpu.make_async_copy(twiddle_hbm, twiddle, in_sem.at[2]),
    ]
    load_traces = pltpu.make_async_copy(traces_hbm, traces, in_sem.at[3])
    load_base = [pltpu.make_async_copy(base_hbm.at[c], base.at[c], in_sem.at[4 + c]) for c in range(CHUNKS)]
    load_table = pltpu.make_async_copy(table_hbm, table, in_sem.at[4 + CHUNKS])
    for load in (load_traces, *small, *load_base, load_table):
        load.start()

    def meet(slot):
        pl.semaphore_wait(here_sem.at[slot], 1)

    def greet():
        peers = sum(jnp.where(exists(step), 1, 0) for step in (1, 2))
        on(exists(1), lambda: pl.semaphore_wait(barrier, peers))
        for slot, step in enumerate((1, 2)):
            on(exists(step), functools.partial(signal, here_sem.at[slot], step))

    def relay():
        meet(1)
        on(exists(2), functools.partial(signal, here_sem.at[2], 2))

    last = depth == 7
    on(last, greet)

    whole[...] = jnp.zeros_like(whole)
    for load in small:
        load.wait()
    whole[0:1, 0:CH] = segment[...] * 2 + live[...]
    packed = whole[...]
    lane = lax.broadcasted_iota(jnp.int32, (8, 128), 1)
    labels[0] = pltpu.roll(packed, HALF, 1)
    labels[1] = jnp.where(lane < HALF, pltpu.roll(packed, 128 - HALF, 1), 0)
    labels[2] = jnp.where((lane >= CH + HALF) & (lane < CH + 2 * HALF), pltpu.roll(packed, CH + HALF, 1), 0)

    def remote(src, dst, send, recv, target):
        return pltpu.make_async_remote_copy(
            src_ref=src, dst_ref=dst, send_sem=send, recv_sem=recv, device_id=(target,), device_id_type=MESH
        )

    def halo(side, piece):
        target = me + 1 if side == 0 else me - 1
        send, recv = halo_send.at[side, piece], halo_recv.at[side, piece]
        if piece == CHUNKS:
            return remote(labels.at[1 + side], labels.at[3 + side], send, recv, target)
        cols = pl.ds(piece * WIDE, WIDE)
        source, place = ((CH, 0), (HALF, CH + HALF))[side]
        return remote(spec.at[pl.ds(source, HALF), cols], spec.at[pl.ds(place, HALF), cols], send, recv, target)

    on(last & exists(1), halo(0, CHUNKS).start)

    load_traces.wait()
    for s in range(spans):
        piece = traces[:, s * SPAN : min(length, (s + 1) * SPAN)]
        if piece.shape[1] < SPAN:
            piece = jnp.concatenate([piece, jnp.zeros((CH, SPAN - piece.shape[1]), jnp.float32)], axis=1)
        top = piece.astype(jnp.bfloat16)
        first[s * CH : (s + 1) * CH, :] = top
        second[s * CH : (s + 1) * CH, :] = (piece - top.astype(jnp.float32)).astype(jnp.bfloat16)
    for c in range(CHUNKS):
        load_base[c].wait()
        parts = []
        for offset in (0, CHUNK):
            cols = slice(offset, offset + CHUNK)
            high, low = base[c, 0, :, cols], base[c, 1, :, cols]
            parts.append(dot(first[...], high) + dot(second[...], high) + dot(first[...], low))
        cosine = twiddle[0:1, c * CHUNK : (c + 1) * CHUNK]
        sine = twiddle[1:2, c * CHUNK : (c + 1) * CHUNK]
        real = parts[0][(spans - 1) * CH :, :]
        imag = parts[1][(spans - 1) * CH :, :]
        for s in range(spans - 2, -1, -1):
            rows = slice(s * CH, (s + 1) * CH)
            real, imag = (
                parts[0][rows, :] + (real * cosine - imag * sine),
                parts[1][rows, :] + (real * sine + imag * cosine),
            )
        spec[HALF : HALF + CH, c * WIDE : c * WIDE + CHUNK] = real
        spec[HALF : HALF + CH, c * WIDE + CHUNK : (c + 1) * WIDE] = imag
        on(last & exists(1), halo(0, c).start)

    def open_right():
        greet()
        for piece in (CHUNKS, *range(CHUNKS)):
            on(exists(1), halo(0, piece).start)

    on(jnp.logical_not(last), open_right)

    on((depth > 0) & exists(-2), relay)

    def send_left():
        meet(0)
        for piece in (CHUNKS, *range(CHUNKS)):
            halo(1, piece).start()

    late = (depth == 0) & (core == 0)
    on(exists(-1) & jnp.logical_not(late), send_left)

    def row_slice(block, half):
        return rows_ref.at[pl.ds(block * CH + half * HALF, HALF)]

    def row_copy(kind, half, source, target_block, target):
        return remote(
            row_slice(source, half), row_slice(target_block, half),
            row_send.at[kind, half], row_recv.at[target_block - 1, half], target,
        )

    def to_sibling(half):
        return row_copy(0, half, 0, 1, me - 1)

    def to_two(half):
        return row_copy(1, half, 0, 2, me - 2)

    def to_four(half):
        return row_copy(2, half, 0, 4, me - 4)

    wide_row = lax.broadcasted_iota(jnp.int32, (CH, 128), 0) + HALF
    wide_lane = lax.broadcasted_iota(jnp.int32, (CH, 128), 1)
    near = jnp.abs(wide_lane - wide_row) <= HALF_WIN
    band_row = lax.broadcasted_iota(jnp.int32, (CHUNK, CHUNK), 0) // BAND
    band_col = lax.broadcasted_iota(jnp.int32, (CHUNK, CHUNK), 1) // BAND
    same = jnp.where(band_row == band_col, 1.0, 0.0).astype(jnp.bfloat16)

    def whiten(half):
        side = half
        there = exists(1) if half == 1 else exists(-1)
        edge = slice(CH + HALF, 2 * CH) if half == 1 else slice(0, HALF)

        def nobody():
            spec[edge, :] = jnp.zeros((HALF, 2 * FB), jnp.float32)
            labels[3 + side] = jnp.zeros((8, 128), jnp.int32)

        on(jnp.logical_not(there), nobody)
        on(there, halo(side, CHUNKS).wait_recv)
        low = half * HALF
        mine = jnp.where(wide_lane == wide_row, labels[0, 0:1, :], 0).astype(jnp.float32)
        mine = jnp.sum(mine, axis=1, keepdims=True).astype(jnp.int32)
        wide = labels[0, 0:1, :] + labels[3 + side, 0:1, :]
        keep = near & ((wide >> 1) == (mine >> 1)) & ((wide & 1) == 1)
        inside = jnp.where(keep, 1.0, 0.0)
        divisor = jnp.maximum(jnp.sum(inside, axis=1, keepdims=True), 1.0)[low : low + HALF]
        alive = (mine & 1).astype(jnp.float32)[low : low + HALF]
        weights = inside[low : low + HALF, low : low + 3 * HALF].astype(jnp.bfloat16)
        weights = jnp.concatenate([weights, weights, weights], axis=1)
        for c in range(CHUNKS):
            on(there, halo(side, c).wait_recv)
            parts = []
            for offset in (c * WIDE, c * WIDE + CHUNK):
                cols = slice(offset, offset + CHUNK)
                stack = jnp.concatenate(split3(spec[low : low + 3 * HALF, cols]), axis=0)
                total = dot(weights, stack)
                value = spec[HALF + low : 2 * HALF + low, cols]
                parts.append(alive * (value * alive - total / divisor))
            square = parts[0] * parts[0] + parts[1] * parts[1]
            sums = dot(jnp.concatenate(split3(square), axis=0), same)
            power = (sums[:HALF] + (sums[HALF : 2 * HALF] + sums[2 * HALF :])) * (1.0 / BAND)
            scale = lax.rsqrt(power + WHITEN_EPS)
            rows_ref[low : low + HALF, c * WIDE : c * WIDE + CHUNK] = (parts[0] * scale).astype(jnp.bfloat16)
            rows_ref[low : low + HALF, c * WIDE + CHUNK : (c + 1) * WIDE] = (parts[1] * scale).astype(jnp.bfloat16)

    def blank(block):
        rows_ref[block * CH : (block + 1) * CH, :] = jnp.zeros((CH, 2 * FB), jnp.bfloat16)

    for block in range(1, REACH + 1):
        on(jnp.logical_not(exists(block)), functools.partial(blank, block))

    def send_early(half):
        on(core == 1, to_sibling(half).start)
        on((depth > 0) & exists(-2), to_two(half).start)
        if half == 1:
            on((depth > 1) & exists(-4), lambda: meet(2))
        on((depth > 1) & exists(-4), to_four(half).start)

    def lower():
        whiten(0)
        send_early(0)

    whiten(1)
    send_early(1)
    on(jnp.logical_not(late), lower)

    def arrived(block, half):
        row_copy(0, half, 0, block, me).wait_recv()

    passed = []

    def forward(block):
        for half in (1, 0):
            on(exists(block), functools.partial(arrived, block, half))
            kind = 3 if block == 2 else 4
            to_low_core_next = row_copy(kind, half, block, block - 1, me + 1)
            on(exists(block) & (core == 0), to_low_core_next.start)
            if block == 2:
                on(exists(block) & (core == 1), row_copy(kind, half, block, 3, me - 1).start)
                passed.append((to_low_core_next, exists(block)))
            else:
                passed.append((to_low_core_next, exists(block) & (core == 0)))

    own = rows_ref[HALF:CH, :].astype(jnp.float32)

    def correlate_upper(block):
        rows = slice(block * CH, (block + 2) * CH)
        for g in range(0, HALF, 16):
            part_ref[g : g + 16, (block - 1) * CH : (block + 1) * CH, :] = correlate(
                own[g : g + 16], lambda cols: rows_ref[rows, cols], table
            )

    forward(2)
    for half in (1, 0):
        on(exists(1), functools.partial(arrived, 1, half))
    load_table.wait()
    correlate_upper(1)

    def catch_up():
        on((depth == 0) & exists(-2), relay)
        on(exists(-4), lambda: meet(2))
        for half in (1, 0):
            @pl.when((half == 1) | jnp.logical_not(late))
            def _():
                on((depth == 0) & exists(-2), to_two(half).start)
                on(exists(-4), to_four(half).start)

    on(exists(-1) & late, send_left)
    on(depth <= 1, catch_up)
    forward(4)
    for half in (1, 0):
        on(exists(3), functools.partial(arrived, 3, half))
    correlate_upper(3)

    def late_lower():
        whiten(0)
        on(exists(-2), to_two(0).start)
        on(exists(-4), to_four(0).start)

    on(late, late_lower)

    for side in (0, 1):
        for piece in range(CHUNKS + 1):
            on(exists(1 - 2 * side), halo(side, piece).wait_send)
    for half in (1, 0):
        on(core == 1, to_sibling(half).wait_send)
        on(exists(-2), to_two(half).wait_send)
        on(exists(-4), to_four(half).wait_send)
    for copy, condition in passed:
        on(condition, copy.wait_send)


GROUP = 8


def finish_kernel(rows_ref, part_ref, table_ref, out_ref):
    step = pl.program_id(0)

    @pl.when(step == 0)
    def _():
        out_ref[...] = part_ref[0:GROUP]

    @pl.when(step == 1)
    def _():
        out_ref[...] = part_ref[GROUP:HALF]

    @pl.when(step >= 2)
    def _():
        own = rows_ref[0:HALF, :].astype(jnp.float32)
        own = jnp.where(step == 2, own[:GROUP], own[GROUP:])
        out_ref[...] = correlate(own, lambda cols: rows_ref[CH:, cols], table_ref)


def on_device(traces, live, segment):
    count = lax.axis_size("fiber")
    channels, length = traces.shape
    base, twiddle, lags = (jnp.asarray(t) for t in tables(length))
    in_hbm = pl.BlockSpec(memory_space=pltpu.HBM)
    in_vmem = pl.BlockSpec(memory_space=pltpu.VMEM)
    spans = -(-length // SPAN)
    rows, part = pl.pallas_call(
        functools.partial(spectra_kernel, count),
        out_shape=(
            jax.ShapeDtypeStruct(((1 + REACH) * channels, 2 * FB), jnp.bfloat16),
            jax.ShapeDtypeStruct((HALF, REACH * channels, LAGS), jnp.bfloat16),
        ),
        in_specs=[in_hbm] * 6,
        out_specs=(in_vmem, in_vmem),
        scratch_shapes=[
            pltpu.VMEM((channels, length), jnp.float32),
            pltpu.VMEM((1, channels), jnp.int32),
            pltpu.VMEM((1, channels), jnp.int32),
            pltpu.VMEM((CHUNKS, 2, SPAN, WIDE), jnp.bfloat16),
            pltpu.VMEM((2, FB), jnp.float32),
            pltpu.VMEM((2 * FB, LAGS), jnp.bfloat16),
            pltpu.VMEM((spans * CH, SPAN), jnp.bfloat16),
            pltpu.VMEM((spans * CH, SPAN), jnp.bfloat16),
            pltpu.VMEM((2 * CH, 2 * FB), jnp.float32),
            pltpu.VMEM((5, 8, 128), jnp.int32),
            pltpu.VMEM((8, 128), jnp.int32),
            pltpu.SemaphoreType.DMA((5 + CHUNKS,)),
            pltpu.SemaphoreType.REGULAR((3,)),
            pltpu.SemaphoreType.DMA((2, CHUNKS + 1)),
            pltpu.SemaphoreType.DMA((2, CHUNKS + 1)),
            pltpu.SemaphoreType.DMA((5, 2)),
            pltpu.SemaphoreType.DMA((4, 2)),
        ],
        compiler_params=pltpu.CompilerParams(
            collective_id=0, has_side_effects=True, vmem_limit_bytes=40 * 1024 * 1024
        ),
        name="spectra",
    )(
        *(
            pltpu.with_memory_space_constraint(x, pltpu.HBM)
            for x in (traces, live.reshape(1, channels), segment.reshape(1, channels), base, twiddle, lags)
        )
    )
    return pl.pallas_call(
        finish_kernel,
        grid=(channels // GROUP,),
        out_shape=jax.ShapeDtypeStruct((channels, REACH * channels, LAGS), jnp.bfloat16),
        in_specs=[in_vmem] * 3,
        out_specs=pl.BlockSpec((GROUP, REACH * channels, LAGS), lambda g: (lax.rem(g + 2, 4), 0, 0)),
        compiler_params=pltpu.CompilerParams(vmem_limit_bytes=40 * 1024 * 1024),
        name="finish",
    )(rows, part, lags)


def solution(mesh):
    return jax.shard_map(
        on_device,
        mesh=mesh,
        in_specs=(P("fiber", None), P("fiber"), P("fiber")),
        out_specs=P("fiber", None, None),
        check_vma=False,
    )
```

time: 33.6 us -> 28.1 us (0.84)
  the two profiles are of different devices: /device:TPU:17 before, /device:TPU:479 now
where the time goes in v2:
time: 28.1 us; the launch traced here: 28 us
  Pallas kernels  27.9 us (99%)
    pallas_call x1, Pallas kernels, on_device(): pl.pallas_call(functools.partial(spectra_kernel, count), out_shape=(jax.S...  24.2 us
    pallas_call x1, Pallas kernels, on_device(): pl.pallas_call(finish_kernel, grid=(channels // GROUP,), out_shape=jax.Sh...  3.72 us

profile of v2, /device:TPU:479, one launch (start us, length us, event | category | flops | bytes accessed | tf_op | source)
XLA Modules:
  0.0 28.0 jit_solution(3639489576841947554)
XLA Ops:
  0.0 0.0 copy-start
  0.0 24.2 %spectra.1 = (bf16[160,1536]{1,0:T(8,128)(2,1)S(1)}, bf16[16,128,256]{2,1,0:T(8,128)(2,1)S(1)}) custom-call(f32[32,3000]{1,0:T(8,128)} %traces_hbm.1, s32[1,32]{1,0:T(1,128)} %bitcast.2, s32[1,32]{1,0:T(1,128)} %bitcast.3, bf16[3,2,256,512]{3,2,1,0:T(8,128)(2,1)} %constant.6.clone.base_hbm, f32[2,768]{1,0:T(2,128)} %constant.7.clone.twiddle_hbm, ...), custom_call_target="tpu_custom_call" | custom-call | tf_op jit(solution)/shard_map/spectra/pallas_call | solution.py:386
  24.2 0.0 copy-done
  24.2 3.7 %finish.1 = bf16[32,128,256]{2,1,0:T(8,128)(2,1)} custom-call(bf16[160,1536]{1,0:T(8,128)(2,1)S(1)} %get-tuple-element.7.rows_ref, bf16[16,128,256]{2,1,0:T(8,128)(2,1)S(1)} %get-tuple-element.8.part_ref, bf16[1536,256]{1,0:T(8,128)(2,1)S(1)} %copy-done), custom_call_target="tpu_custom_call" | custom-call | tf_op jit(solution)/shard_map/finish/pallas_call | solution.py:423
Async XLA Ops:
  0.0 24.2 %copy-start = (bf16[1536,256]{1,0:T(8,128)(2,1)S(1)}, bf16[1536,256]{1,0:T(8,128)(2,1)}, u32[]{:S(2)}) copy-start(bf16[1536,256]{1,0:T(8,128)(2,1)} %constant.8.clone.table_hbm.table_ref) | copy-start | bytes 2359300

commit v3 on v2

--- a/solution.py
+++ b/solution.py
@@ -63,28 +63,32 @@
     return jnp.dot(a, b, preferred_element_type=jnp.float32)
 
 
-def correlate(own, far, table_ref):
+def columns(start, width=CHUNK):
+    return pl.ds(start if isinstance(start, int) else pl.multiple_of(start, CHUNK), width)
+
+
+def correlate(own, far, table_ref, shape):
     total = None
     for c in range(CHUNKS):
         re_cols = slice(c * WIDE, c * WIDE + CHUNK)
         im_cols = slice(c * WIDE + CHUNK, (c + 1) * WIDE)
-        own_re = own[:, None, re_cols]
-        own_im = own[:, None, im_cols]
+        own_re = own(re_cols)[:, None]
+        own_im = own(im_cols)[:, None]
         far_re = far(re_cols).astype(jnp.float32)[None]
         far_im = far(im_cols).astype(jnp.float32)[None]
-        shape = (own.shape[0] * far_re.shape[1], CHUNK)
-        real = (own_re * far_re + own_im * far_im).astype(jnp.bfloat16).reshape(shape)
-        imag = (own_im * far_re - own_re * far_im).astype(jnp.bfloat16).reshape(shape)
+        flat = (own_re.shape[0] * far_re.shape[1], CHUNK)
+        real = (own_re * far_re + own_im * far_im).astype(jnp.bfloat16).reshape(flat)
+        imag = (own_im * far_re - own_re * far_im).astype(jnp.bfloat16).reshape(flat)
         term = dot(real, table_ref[re_cols, :]) + dot(imag, table_ref[im_cols, :])
         total = term if total is None else total + term
-    return total.astype(jnp.bfloat16).reshape(own.shape[0], -1, LAGS)
+    return total.astype(jnp.bfloat16).reshape(shape)
 
 
 def spectra_kernel(
     count,
     traces_hbm, live_hbm, segment_hbm, base_hbm, twiddle_hbm, table_hbm,
     rows_ref, part_ref,
-    traces, live, segment, base, twiddle, table, first, second, spec, labels, whole,
+    traces, live, segment, base, twiddle, table, first, second, spec, labels, whole, own,
     in_sem, here_sem, halo_send, halo_recv, row_send, row_recv,
 ):
     me = lax.axis_index("fiber")
@@ -152,9 +156,9 @@
     def halo(side, piece):
         target = me + 1 if side == 0 else me - 1
         send, recv = halo_send.at[side, piece], halo_recv.at[side, piece]
-        if piece == CHUNKS:
+        if isinstance(piece, int) and piece == CHUNKS:
             return remote(labels.at[1 + side], labels.at[3 + side], send, recv, target)
-        cols = pl.ds(piece * WIDE, WIDE)
+        cols = columns(piece * WIDE, WIDE)
         source, place = ((CH, 0), (HALF, CH + HALF))[side]
         return remote(spec.at[pl.ds(source, HALF), cols], spec.at[pl.ds(place, HALF), cols], send, recv, target)
 
@@ -168,15 +172,15 @@
         top = piece.astype(jnp.bfloat16)
         first[s * CH : (s + 1) * CH, :] = top
         second[s * CH : (s + 1) * CH, :] = (piece - top.astype(jnp.float32)).astype(jnp.bfloat16)
-    for c in range(CHUNKS):
-        load_base[c].wait()
+
+    def transform(c, carry):
+        pltpu.make_async_copy(base_hbm.at[c], base.at[c], in_sem.at[4 + c]).wait()
         parts = []
         for offset in (0, CHUNK):
-            cols = slice(offset, offset + CHUNK)
-            high, low = base[c, 0, :, cols], base[c, 1, :, cols]
+            high, low = (base[c, k, :, offset : offset + CHUNK] for k in (0, 1))
             parts.append(dot(first[...], high) + dot(second[...], high) + dot(first[...], low))
-        cosine = twiddle[0:1, c * CHUNK : (c + 1) * CHUNK]
-        sine = twiddle[1:2, c * CHUNK : (c + 1) * CHUNK]
+        cosine = twiddle[0:1, columns(c * CHUNK)]
+        sine = twiddle[1:2, columns(c * CHUNK)]
         real = parts[0][(spans - 1) * CH :, :]
         imag = parts[1][(spans - 1) * CH :, :]
         for s in range(spans - 2, -1, -1):
@@ -185,9 +189,12 @@
                 parts[0][rows, :] + (real * cosine - imag * sine),
                 parts[1][rows, :] + (real * sine + imag * cosine),
             )
-        spec[HALF : HALF + CH, c * WIDE : c * WIDE + CHUNK] = real
-        spec[HALF : HALF + CH, c * WIDE + CHUNK : (c + 1) * WIDE] = imag
+        spec[HALF : HALF + CH, columns(c * WIDE)] = real
+        spec[HALF : HALF + CH, columns(c * WIDE + CHUNK)] = imag
         on(last & exists(1), halo(0, c).start)
+        return carry
+
+    lax.fori_loop(0, CHUNKS, transform, 0)
 
     def open_right():
         greet()
@@ -224,49 +231,51 @@
     def to_four(half):
         return row_copy(2, half, 0, 4, me - 4)
 
-    wide_row = lax.broadcasted_iota(jnp.int32, (CH, 128), 0) + HALF
-    wide_lane = lax.broadcasted_iota(jnp.int32, (CH, 128), 1)
-    near = jnp.abs(wide_lane - wide_row) <= HALF_WIN
+    wide_row = lax.broadcasted_iota(jnp.int32, (HALF, 128), 0) + HALF
+    wide_lane = lax.broadcasted_iota(jnp.int32, (HALF, 128), 1)
     band_row = lax.broadcasted_iota(jnp.int32, (CHUNK, CHUNK), 0) // BAND
     band_col = lax.broadcasted_iota(jnp.int32, (CHUNK, CHUNK), 1) // BAND
-    same = jnp.where(band_row == band_col, 1.0, 0.0).astype(jnp.bfloat16)
 
     def whiten(half):
-        side = half
-        there = exists(1) if half == 1 else exists(-1)
-        edge = slice(CH + HALF, 2 * CH) if half == 1 else slice(0, HALF)
-
-        def nobody():
-            spec[edge, :] = jnp.zeros((HALF, 2 * FB), jnp.float32)
-            labels[3 + side] = jnp.zeros((8, 128), jnp.int32)
-
-        on(jnp.logical_not(there), nobody)
-        on(there, halo(side, CHUNKS).wait_recv)
-        low = half * HALF
-        mine = jnp.where(wide_lane == wide_row, labels[0, 0:1, :], 0).astype(jnp.float32)
+        there = ((half == 1) & exists(1)) | ((half == 0) & exists(-1))
+        low = pl.multiple_of(half * HALF, HALF)
+
+        @pl.when(there)
+        def _():
+            for piece in (CHUNKS, *range(CHUNKS)):
+                on(half == 0, halo(0, piece).wait_recv)
+                on(half == 1, halo(1, piece).wait_recv)
+
+        @pl.when(jnp.logical_not(there))
+        def _():
+            spec[pl.ds(pl.multiple_of(half * (CH + HALF), HALF), HALF), :] = jnp.zeros((HALF, 2 * FB), jnp.float32)
+            labels[3 + half] = jnp.zeros((8, 128), jnp.int32)
+
+        place = wide_row + low
+        mine = jnp.where(wide_lane == place, labels[0, 0:1, :], 0).astype(jnp.float32)
         mine = jnp.sum(mine, axis=1, keepdims=True).astype(jnp.int32)
-        wide = labels[0, 0:1, :] + labels[3 + side, 0:1, :]
-        keep = near & ((wide >> 1) == (mine >> 1)) & ((wide & 1) == 1)
+        wide = labels[0, 0:1, :] + labels[3 + half, 0:1, :]
+        keep = (jnp.abs(wide_lane - place) <= HALF_WIN) & ((wide >> 1) == (mine >> 1)) & ((wide & 1) == 1)
         inside = jnp.where(keep, 1.0, 0.0)
-        divisor = jnp.maximum(jnp.sum(inside, axis=1, keepdims=True), 1.0)[low : low + HALF]
-        alive = (mine & 1).astype(jnp.float32)[low : low + HALF]
-        weights = inside[low : low + HALF, low : low + 3 * HALF].astype(jnp.bfloat16)
+        divisor = jnp.maximum(jnp.sum(inside, axis=1, keepdims=True), 1.0)
+        alive = (mine & 1).astype(jnp.float32)
+        weights = jnp.where(half == 1, pltpu.roll(inside, 128 - HALF, 1), inside)[:, : 3 * HALF].astype(jnp.bfloat16)
         weights = jnp.concatenate([weights, weights, weights], axis=1)
+        same = jnp.where(band_row == band_col, 1.0, 0.0).astype(jnp.bfloat16)
         for c in range(CHUNKS):
-            on(there, halo(side, c).wait_recv)
             parts = []
             for offset in (c * WIDE, c * WIDE + CHUNK):
                 cols = slice(offset, offset + CHUNK)
-                stack = jnp.concatenate(split3(spec[low : low + 3 * HALF, cols]), axis=0)
-                total = dot(weights, stack)
-                value = spec[HALF + low : 2 * HALF + low, cols]
-                parts.append(alive * (value * alive - total / divisor))
+                stack = jnp.concatenate(split3(spec[pl.ds(low, 3 * HALF), cols]), axis=0)
+                sums = dot(weights, stack)
+                value = spec[pl.ds(pl.multiple_of(HALF + low, HALF), HALF), cols]
+                parts.append(alive * (value * alive - sums / divisor))
             square = parts[0] * parts[0] + parts[1] * parts[1]
             sums = dot(jnp.concatenate(split3(square), axis=0), same)
             power = (sums[:HALF] + (sums[HALF : 2 * HALF] + sums[2 * HALF :])) * (1.0 / BAND)
             scale = lax.rsqrt(power + WHITEN_EPS)
-            rows_ref[low : low + HALF, c * WIDE : c * WIDE + CHUNK] = (parts[0] * scale).astype(jnp.bfloat16)
-            rows_ref[low : low + HALF, c * WIDE + CHUNK : (c + 1) * WIDE] = (parts[1] * scale).astype(jnp.bfloat16)
+            rows_ref[pl.ds(low, HALF), c * WIDE : c * WIDE + CHUNK] = (parts[0] * scale).astype(jnp.bfloat16)
+            rows_ref[pl.ds(low, HALF), c * WIDE + CHUNK : (c + 1) * WIDE] = (parts[1] * scale).astype(jnp.bfloat16)
 
     def blank(block):
         rows_ref[block * CH : (block + 1) * CH, :] = jnp.zeros((CH, 2 * FB), jnp.bfloat16)
@@ -274,52 +283,18 @@
     for block in range(1, REACH + 1):
         on(jnp.logical_not(exists(block)), functools.partial(blank, block))
 
-    def send_early(half):
-        on(core == 1, to_sibling(half).start)
-        on((depth > 0) & exists(-2), to_two(half).start)
-        if half == 1:
-            on((depth > 1) & exists(-4), lambda: meet(2))
-        on((depth > 1) & exists(-4), to_four(half).start)
-
-    def lower():
-        whiten(0)
-        send_early(0)
-
-    whiten(1)
-    send_early(1)
-    on(jnp.logical_not(late), lower)
-
     def arrived(block, half):
         row_copy(0, half, 0, block, me).wait_recv()
 
-    passed = []
+    def to_next(block, half):
+        return row_copy(3 if block == 2 else 4, half, block, block - 1, me + 1)
 
     def forward(block):
         for half in (1, 0):
             on(exists(block), functools.partial(arrived, block, half))
-            kind = 3 if block == 2 else 4
-            to_low_core_next = row_copy(kind, half, block, block - 1, me + 1)
-            on(exists(block) & (core == 0), to_low_core_next.start)
+            on(exists(block) & (core == 0), to_next(block, half).start)
             if block == 2:
-                on(exists(block) & (core == 1), row_copy(kind, half, block, 3, me - 1).start)
-                passed.append((to_low_core_next, exists(block)))
-            else:
-                passed.append((to_low_core_next, exists(block) & (core == 0)))
-
-    own = rows_ref[HALF:CH, :].astype(jnp.float32)
-
-    def correlate_upper(block):
-        rows = slice(block * CH, (block + 2) * CH)
-        for g in range(0, HALF, 16):
-            part_ref[g : g + 16, (block - 1) * CH : (block + 1) * CH, :] = correlate(
-                own[g : g + 16], lambda cols: rows_ref[rows, cols], table
-            )
-
-    forward(2)
-    for half in (1, 0):
-        on(exists(1), functools.partial(arrived, 1, half))
-    load_table.wait()
-    correlate_upper(1)
+                on(exists(block) & (core == 1), row_copy(3, half, block, 3, me - 1).start)
 
     def catch_up():
         on((depth == 0) & exists(-2), relay)
@@ -330,19 +305,43 @@
                 on((depth == 0) & exists(-2), to_two(half).start)
                 on(exists(-4), to_four(half).start)
 
-    on(exists(-1) & late, send_left)
-    on(depth <= 1, catch_up)
-    forward(4)
-    for half in (1, 0):
-        on(exists(3), functools.partial(arrived, 3, half))
-    correlate_upper(3)
-
-    def late_lower():
-        whiten(0)
-        on(exists(-2), to_two(0).start)
-        on(exists(-4), to_four(0).start)
-
-    on(late, late_lower)
+    def stage(t, carry):
+        @pl.when((t == 0) | ((t == 1) & jnp.logical_not(late)) | ((t == 4) & late))
+        def _():
+            half = jnp.where(t == 0, 1, 0)
+            whiten(half)
+            on(core == 1, to_sibling(half).start)
+            on(((depth > 0) | (t == 4)) & exists(-2), to_two(half).start)
+            on((depth > 1) & (t == 0) & exists(-4), lambda: meet(2))
+            on(((depth > 1) | (t == 4)) & exists(-4), to_four(half).start)
+
+        @pl.when((t == 2) | (t == 3))
+        def _():
+            @pl.when(t == 2)
+            def _():
+                forward(2)
+                for half in (1, 0):
+                    on(exists(1), functools.partial(arrived, 1, half))
+                load_table.wait()
+                own[...] = rows_ref[HALF:CH, :].astype(jnp.float32)
+
+            @pl.when(t == 3)
+            def _():
+                on(exists(-1) & late, send_left)
+                on(depth <= 1, catch_up)
+                forward(4)
+                for half in (1, 0):
+                    on(exists(3), functools.partial(arrived, 3, half))
+
+            pair = t - 2
+            far_rows = pl.ds(pl.multiple_of(CH + pair * 2 * CH, CH), 2 * CH)
+            part_ref[:, pl.ds(pl.multiple_of(pair * 2 * CH, CH), 2 * CH), :] = correlate(
+                lambda cols: own[:, cols], lambda cols: rows_ref[far_rows, cols], table, (HALF, 2 * CH, LAGS)
+            )
+
+        return carry
+
+    lax.fori_loop(0, 5, stage, 0)
 
     for side in (0, 1):
         for piece in range(CHUNKS + 1):
@@ -351,29 +350,35 @@
         on(core == 1, to_sibling(half).wait_send)
         on(exists(-2), to_two(half).wait_send)
         on(exists(-4), to_four(half).wait_send)
-    for copy, condition in passed:
-        on(condition, copy.wait_send)
+    for half in (1, 0):
+        on(exists(2), to_next(2, half).wait_send)
+        on(exists(4) & (core == 0), to_next(4, half).wait_send)
 
 
 GROUP = 8
 
 
-def finish_kernel(rows_ref, part_ref, table_ref, out_ref):
-    step = pl.program_id(0)
-
-    @pl.when(step == 0)
-    def _():
-        out_ref[...] = part_ref[0:GROUP]
-
-    @pl.when(step == 1)
-    def _():
-        out_ref[...] = part_ref[GROUP:HALF]
-
-    @pl.when(step >= 2)
-    def _():
-        own = rows_ref[0:HALF, :].astype(jnp.float32)
-        own = jnp.where(step == 2, own[:GROUP], own[GROUP:])
-        out_ref[...] = correlate(own, lambda cols: rows_ref[CH:, cols], table_ref)
+def finish_kernel(rows_ref, part_ref, table_ref, out_ref, own, done, sem):
+    upper = pltpu.make_async_copy(part_ref, out_ref.at[pl.ds(HALF, HALF)], sem.at[0])
+    upper.start()
+    own[...] = rows_ref[0:HALF, :].astype(jnp.float32)
+
+    def lower(p):
+        rows = pl.ds(pl.multiple_of(p * GROUP, GROUP), GROUP)
+        return rows, pltpu.make_async_copy(done.at[rows], out_ref.at[rows], sem.at[1 + p])
+
+    def step(p, carry):
+        rows, copy = lower(p)
+        done[rows] = correlate(
+            lambda cols: own[rows, cols], lambda cols: rows_ref[CH:, cols], table_ref, (GROUP, REACH * CH, LAGS)
+        )
+        copy.start()
+        return carry
+
+    lax.fori_loop(0, HALF // GROUP, step, 0)
+    upper.wait()
+    for p in range(HALF // GROUP):
+        lower(p)[1].wait()
 
 
 def on_device(traces, live, segment):
@@ -403,6 +408,7 @@
             pltpu.VMEM((2 * CH, 2 * FB), jnp.float32),
             pltpu.VMEM((5, 8, 128), jnp.int32),
             pltpu.VMEM((8, 128), jnp.int32),
+            pltpu.VMEM((HALF, 2 * FB), jnp.float32),
             pltpu.SemaphoreType.DMA((5 + CHUNKS,)),
             pltpu.SemaphoreType.REGULAR((3,)),
             pltpu.SemaphoreType.DMA((2, CHUNKS + 1)),
@@ -422,10 +428,14 @@
     )
     return pl.pallas_call(
         finish_kernel,
-        grid=(channels // GROUP,),
         out_shape=jax.ShapeDtypeStruct((channels, REACH * channels, LAGS), jnp.bfloat16),
         in_specs=[in_vmem] * 3,
-        out_specs=pl.BlockSpec((GROUP, REACH * channels, LAGS), lambda g: (lax.rem(g + 2, 4), 0, 0)),
+        out_specs=in_hbm,
+        scratch_shapes=[
+            pltpu.VMEM((HALF, 2 * FB), jnp.float32),
+            pltpu.VMEM((HALF, REACH * CH, LAGS), jnp.bfloat16),
+            pltpu.SemaphoreType.DMA((1 + HALF // GROUP,)),
+        ],
         compiler_params=pltpu.CompilerParams(vmem_limit_bytes=40 * 1024 * 1024),
         name="finish",
     )(rows, part, lags)

time: 28.1 us -> 25.5 us (0.907)
  the two profiles are of different devices: /device:TPU:479 before, /device:TPU:1 now
where the time goes in v3:
time: 25.5 us; the launch traced here: 25.4 us
  Pallas kernels  25.3 us (99%)
    pallas_call x1, Pallas kernels, on_device(): pl.pallas_call(functools.partial(spectra_kernel, count), out_shape=(jax.S...  22.5 us
    pallas_call x1, Pallas kernels, on_device(): pl.pallas_call(finish_kernel, out_shape=jax.ShapeDtypeStruct((channels, R...  2.85 us

profile of v3, /device:TPU:1, one launch (start us, length us, event | category | flops | bytes accessed | tf_op | source)
XLA Modules:
  0.0 25.4 jit_solution(2416790726242827835)
XLA Ops:
  0.0 0.0 copy-start
  0.0 22.5 %spectra.1 = (bf16[160,1536]{1,0:T(8,128)(2,1)S(1)}, bf16[16,128,256]{2,1,0:T(8,128)(2,1)S(1)}) custom-call(f32[32,3000]{1,0:T(8,128)} %traces_hbm.1, s32[1,32]{1,0:T(1,128)} %bitcast.2, s32[1,32]{1,0:T(1,128)} %bitcast.3, bf16[3,2,256,512]{3,2,1,0:T(8,128)(2,1)} %constant.6.clone.base_hbm, f32[2,768]{1,0:T(2,128)} %constant.7.clone.twiddle_hbm, ...), custom_call_target="tpu_custom_call" | custom-call | tf_op jit(solution)/shard_map/spectra/pallas_call | solution.py:391
  22.5 0.0 copy-done
  22.5 2.9 %finish.1 = bf16[32,128,256]{2,1,0:T(8,128)(2,1)} custom-call(bf16[160,1536]{1,0:T(8,128)(2,1)S(1)} %get-tuple-element.7.rows_ref, bf16[16,128,256]{2,1,0:T(8,128)(2,1)S(1)} %get-tuple-element.8.part_ref, bf16[1536,256]{1,0:T(8,128)(2,1)S(1)} %copy-done), custom_call_target="tpu_custom_call" | custom-call | tf_op jit(solution)/shard_map/finish/pallas_call | solution.py:429
Async XLA Ops:
  0.0 22.5 %copy-start = (bf16[1536,256]{1,0:T(8,128)(2,1)S(1)}, bf16[1536,256]{1,0:T(8,128)(2,1)}, u32[]{:S(2)}) copy-start(bf16[1536,256]{1,0:T(8,128)(2,1)} %constant.8.clone.table_hbm.table_ref) | copy-start | bytes 2359300

commit v4 on v3

--- a/solution.py
+++ b/solution.py
@@ -110,6 +110,7 @@
 
     for step in (1, 2):
         on(exists(-step), functools.partial(signal, barrier, -step))
+    on((depth < 7) & exists(2), functools.partial(signal, barrier, 2))
 
     small = [
         pltpu.make_async_copy(live_hbm, live, in_sem.at[0]),
@@ -126,17 +127,17 @@
         pl.semaphore_wait(here_sem.at[slot], 1)
 
     def greet():
-        peers = sum(jnp.where(exists(step), 1, 0) for step in (1, 2))
-        on(exists(1), lambda: pl.semaphore_wait(barrier, peers))
-        for slot, step in enumerate((1, 2)):
-            on(exists(step), functools.partial(signal, here_sem.at[slot], step))
+        awaited = (exists(1), exists(2), (depth > 0) & exists(-2))
+        peers = sum(jnp.where(peer, 1, 0) for peer in awaited)
+        on(peers > 0, lambda: pl.semaphore_wait(barrier, peers))
+        on(exists(1), functools.partial(signal, here_sem.at[0], 1))
+        on((depth == 7) & exists(2), functools.partial(signal, here_sem.at[1], 2))
+        on(depth > 0, relay)
 
     def relay():
-        meet(1)
-        on(exists(2), functools.partial(signal, here_sem.at[2], 2))
+        on(exists(-2) & exists(2), functools.partial(signal, here_sem.at[2], 2))
 
     last = depth == 7
-    on(last, greet)
 
     whole[...] = jnp.zeros_like(whole)
     for load in small:
@@ -162,8 +163,6 @@
         source, place = ((CH, 0), (HALF, CH + HALF))[side]
         return remote(spec.at[pl.ds(source, HALF), cols], spec.at[pl.ds(place, HALF), cols], send, recv, target)
 
-    on(last & exists(1), halo(0, CHUNKS).start)
-
     load_traces.wait()
     for s in range(spans):
         piece = traces[:, s * SPAN : min(length, (s + 1) * SPAN)]
@@ -172,6 +171,12 @@
         top = piece.astype(jnp.bfloat16)
         first[s * CH : (s + 1) * CH, :] = top
         second[s * CH : (s + 1) * CH, :] = (piece - top.astype(jnp.float32)).astype(jnp.bfloat16)
+
+    def greet_first():
+        greet()
+        on(exists(1), halo(0, CHUNKS).start)
+
+    on(last, greet_first)
 
     def transform(c, carry):
         pltpu.make_async_copy(base_hbm.at[c], base.at[c], in_sem.at[4 + c]).wait()
@@ -202,8 +207,6 @@
             on(exists(1), halo(0, piece).start)
 
     on(jnp.logical_not(last), open_right)
-
-    on((depth > 0) & exists(-2), relay)
 
     def send_left():
         meet(0)
@@ -274,8 +277,10 @@
             sums = dot(jnp.concatenate(split3(square), axis=0), same)
             power = (sums[:HALF] + (sums[HALF : 2 * HALF] + sums[2 * HALF :])) * (1.0 / BAND)
             scale = lax.rsqrt(power + WHITEN_EPS)
-            rows_ref[pl.ds(low, HALF), c * WIDE : c * WIDE + CHUNK] = (parts[0] * scale).astype(jnp.bfloat16)
-            rows_ref[pl.ds(low, HALF), c * WIDE + CHUNK : (c + 1) * WIDE] = (parts[1] * scale).astype(jnp.bfloat16)
+            for part, offset in zip(parts, (c * WIDE, c * WIDE + CHUNK)):
+                white = (part * scale).astype(jnp.bfloat16)
+                rows_ref[pl.ds(low, HALF), offset : offset + CHUNK] = white
+                own[pl.ds(low, HALF), offset : offset + CHUNK] = white.astype(jnp.float32)
 
     def blank(block):
         rows_ref[block * CH : (block + 1) * CH, :] = jnp.zeros((CH, 2 * FB), jnp.bfloat16)
@@ -297,7 +302,11 @@
                 on(exists(block) & (core == 1), row_copy(3, half, block, 3, me - 1).start)
 
     def catch_up():
-        on((depth == 0) & exists(-2), relay)
+        def relay_late():
+            meet(1)
+            relay()
+
+        on((depth == 0) & exists(-2), relay_late)
         on(exists(-4), lambda: meet(2))
         for half in (1, 0):
             @pl.when((half == 1) | jnp.logical_not(late))
@@ -305,17 +314,19 @@
                 on((depth == 0) & exists(-2), to_two(half).start)
                 on(exists(-4), to_four(half).start)
 
+    early = jnp.logical_not(late)
+
     def stage(t, carry):
-        @pl.when((t == 0) | ((t == 1) & jnp.logical_not(late)) | ((t == 4) & late))
+        @pl.when((t == 0) | ((t == 1) & early) | ((t == 5) & late))
         def _():
-            half = jnp.where(t == 0, 1, 0)
+            half = jnp.where((t == 1) | ((t == 0) & late), 1, 0)
             whiten(half)
             on(core == 1, to_sibling(half).start)
-            on(((depth > 0) | (t == 4)) & exists(-2), to_two(half).start)
+            on(((depth > 0) | (t == 5)) & exists(-2), to_two(half).start)
             on((depth > 1) & (t == 0) & exists(-4), lambda: meet(2))
-            on(((depth > 1) | (t == 4)) & exists(-4), to_four(half).start)
-
-        @pl.when((t == 2) | (t == 3))
+            on(((depth > 1) | (t == 5)) & exists(-4), to_four(half).start)
+
+        @pl.when((t == 2) | ((t == 3) & early) | (t == 4) | ((t >= 6) & late))
         def _():
             @pl.when(t == 2)
             def _():
@@ -323,9 +334,8 @@
                 for half in (1, 0):
                     on(exists(1), functools.partial(arrived, 1, half))
                 load_table.wait()
-                own[...] = rows_ref[HALF:CH, :].astype(jnp.float32)
-
-            @pl.when(t == 3)
+
+            @pl.when(t == 4)
             def _():
                 on(exists(-1) & late, send_left)
                 on(depth <= 1, catch_up)
@@ -333,15 +343,17 @@
                 for half in (1, 0):
                     on(exists(3), functools.partial(arrived, 3, half))
 
-            pair = t - 2
+            half = jnp.where((t == 2) | (t == 4), 1, 0)
+            pair = jnp.where((t == 4) | (t == 7), 1, 0)
+            near_rows = pl.ds(pl.multiple_of(half * HALF, HALF), HALF)
             far_rows = pl.ds(pl.multiple_of(CH + pair * 2 * CH, CH), 2 * CH)
-            part_ref[:, pl.ds(pl.multiple_of(pair * 2 * CH, CH), 2 * CH), :] = correlate(
-                lambda cols: own[:, cols], lambda cols: rows_ref[far_rows, cols], table, (HALF, 2 * CH, LAGS)
+            part_ref[near_rows, pl.ds(pl.multiple_of(pair * 2 * CH, CH), 2 * CH), :] = correlate(
+                lambda cols: own[near_rows, cols], lambda cols: rows_ref[far_rows, cols], table, (HALF, 2 * CH, LAGS)
             )
 
         return carry
 
-    lax.fori_loop(0, 5, stage, 0)
+    lax.fori_loop(0, jnp.where(late, 8, 5), stage, 0)
 
     for side in (0, 1):
         for piece in range(CHUNKS + 1):
@@ -355,30 +367,32 @@
         on(exists(4) & (core == 0), to_next(4, half).wait_send)
 
 
-GROUP = 8
-
-
-def finish_kernel(rows_ref, part_ref, table_ref, out_ref, own, done, sem):
-    upper = pltpu.make_async_copy(part_ref, out_ref.at[pl.ds(HALF, HALF)], sem.at[0])
+def finish_kernel(rows_ref, part_ref, table_ref, out_ref, done, sem):
+    me = lax.axis_index("fiber")
+    late = (lax.rem(me, 2) == 0) & (lax.rem(me // 2, 8) == 0)
+    below, above = pl.ds(0, HALF), pl.ds(HALF, HALF)
+    first, second = pl.ds(0, 2 * CH), pl.ds(2 * CH, 2 * CH)
+    upper = pltpu.make_async_copy(part_ref.at[above], out_ref.at[above], sem.at[0])
+    lower = pltpu.make_async_copy(part_ref.at[below, first], out_ref.at[below, first], sem.at[1])
+    rest = pltpu.make_async_copy(done, out_ref.at[below, second], sem.at[2])
+    rest_there = pltpu.make_async_copy(part_ref.at[below, second], out_ref.at[below, second], sem.at[2])
     upper.start()
-    own[...] = rows_ref[0:HALF, :].astype(jnp.float32)
-
-    def lower(p):
-        rows = pl.ds(pl.multiple_of(p * GROUP, GROUP), GROUP)
-        return rows, pltpu.make_async_copy(done.at[rows], out_ref.at[rows], sem.at[1 + p])
-
-    def step(p, carry):
-        rows, copy = lower(p)
-        done[rows] = correlate(
-            lambda cols: own[rows, cols], lambda cols: rows_ref[CH:, cols], table_ref, (GROUP, REACH * CH, LAGS)
+    lower.start()
+    pl.when(late)(rest_there.start)
+
+    @pl.when(jnp.logical_not(late))
+    def _():
+        done[...] = correlate(
+            lambda cols: rows_ref[below, cols].astype(jnp.float32),
+            lambda cols: rows_ref[3 * CH :, cols],
+            table_ref,
+            (HALF, 2 * CH, LAGS),
         )
-        copy.start()
-        return carry
-
-    lax.fori_loop(0, HALF // GROUP, step, 0)
+        rest.start()
+
     upper.wait()
-    for p in range(HALF // GROUP):
-        lower(p)[1].wait()
+    lower.wait()
+    rest.wait()
 
 
 def on_device(traces, live, segment):
@@ -392,7 +406,7 @@
         functools.partial(spectra_kernel, count),
         out_shape=(
             jax.ShapeDtypeStruct(((1 + REACH) * channels, 2 * FB), jnp.bfloat16),
-            jax.ShapeDtypeStruct((HALF, REACH * channels, LAGS), jnp.bfloat16),
+            jax.ShapeDtypeStruct((channels, REACH * channels, LAGS), jnp.bfloat16),
         ),
         in_specs=[in_hbm] * 6,
         out_specs=(in_vmem, in_vmem),
@@ -408,7 +422,7 @@
             pltpu.VMEM((2 * CH, 2 * FB), jnp.float32),
             pltpu.VMEM((5, 8, 128), jnp.int32),
             pltpu.VMEM((8, 128), jnp.int32),
-            pltpu.VMEM((HALF, 2 * FB), jnp.float32),
+            pltpu.VMEM((CH, 2 * FB), jnp.float32),
             pltpu.SemaphoreType.DMA((5 + CHUNKS,)),
             pltpu.SemaphoreType.REGULAR((3,)),
             pltpu.SemaphoreType.DMA((2, CHUNKS + 1)),
@@ -432,9 +446,8 @@
         in_specs=[in_vmem] * 3,
         out_specs=in_hbm,
         scratch_shapes=[
-            pltpu.VMEM((HALF, 2 * FB), jnp.float32),
-            pltpu.VMEM((HALF, REACH * CH, LAGS), jnp.bfloat16),
-            pltpu.SemaphoreType.DMA((1 + HALF // GROUP,)),
+            pltpu.VMEM((HALF, 2 * CH, LAGS), jnp.bfloat16),
+            pltpu.SemaphoreType.DMA((3,)),
         ],
         compiler_params=pltpu.CompilerParams(vmem_limit_bytes=40 * 1024 * 1024),
         name="finish",

time: 25.5 us -> 24.1 us (0.945)
  the two profiles are of different devices: /device:TPU:1 before, /device:TPU:479 now
where the time goes in v4:
time: 24.1 us; the launch traced here: 24 us
  Pallas kernels  24 us (100%)
    pallas_call x1, Pallas kernels, on_device(): pl.pallas_call(functools.partial(spectra_kernel, count), out_shape=(jax.S...  22.1 us
    pallas_call x1, Pallas kernels, on_device(): pl.pallas_call(finish_kernel, out_shape=jax.ShapeDtypeStruct((channels, R...  1.85 us

profile of v4, /device:TPU:479, one launch (start us, length us, event | category | flops | bytes accessed | tf_op | source)
XLA Modules:
  0.0 24.0 jit_solution(1320057754134745117)
XLA Ops:
  0.0 0.0 copy-start
  0.0 22.1 %spectra.1 = (bf16[160,1536]{1,0:T(8,128)(2,1)S(1)}, bf16[32,128,256]{2,1,0:T(8,128)(2,1)S(1)}) custom-call(f32[32,3000]{1,0:T(8,128)} %traces_hbm.1, s32[1,32]{1,0:T(1,128)} %bitcast.2, s32[1,32]{1,0:T(1,128)} %bitcast.3, bf16[3,2,256,512]{3,2,1,0:T(8,128)(2,1)} %constant.6.clone.base_hbm, f32[2,768]{1,0:T(2,128)} %constant.7.clone.twiddle_hbm, ...), custom_call_target="tpu_custom_call" | custom-call | tf_op jit(solution)/shard_map/spectra/pallas_call | solution.py:405
  22.1 0.0 copy-done
  22.1 1.9 %finish.1 = bf16[32,128,256]{2,1,0:T(8,128)(2,1)} custom-call(bf16[160,1536]{1,0:T(8,128)(2,1)S(1)} %get-tuple-element.7.rows_ref, bf16[32,128,256]{2,1,0:T(8,128)(2,1)S(1)} %get-tuple-element.8.part_ref, bf16[1536,256]{1,0:T(8,128)(2,1)S(1)} %copy-done), custom_call_target="tpu_custom_call" | custom-call | tf_op jit(solution)/shard_map/finish/pallas_call | solution.py:443
Async XLA Ops:
  0.0 22.1 %copy-start = (bf16[1536,256]{1,0:T(8,128)(2,1)S(1)}, bf16[1536,256]{1,0:T(8,128)(2,1)}, u32[]{:S(2)}) copy-start(bf16[1536,256]{1,0:T(8,128)(2,1)} %constant.8.clone.table_hbm.table_ref) | copy-start | bytes 2359300

commit v5 on v4

--- a/solution.py
+++ b/solution.py
@@ -132,10 +132,6 @@
         on(peers > 0, lambda: pl.semaphore_wait(barrier, peers))
         on(exists(1), functools.partial(signal, here_sem.at[0], 1))
         on((depth == 7) & exists(2), functools.partial(signal, here_sem.at[1], 2))
-        on(depth > 0, relay)
-
-    def relay():
-        on(exists(-2) & exists(2), functools.partial(signal, here_sem.at[2], 2))
 
     last = depth == 7
 
@@ -232,7 +228,10 @@
         return row_copy(1, half, 0, 2, me - 2)
 
     def to_four(half):
-        return row_copy(2, half, 0, 4, me - 4)
+        return row_copy(5, half, 0, 4, me - 4)
+
+    def pass_on(half):
+        return row_copy(2, half, 2, 4, me - 2)
 
     wide_row = lax.broadcasted_iota(jnp.int32, (HALF, 128), 0) + HALF
     wide_lane = lax.broadcasted_iota(jnp.int32, (HALF, 128), 1)
@@ -295,24 +294,23 @@
         return row_copy(3 if block == 2 else 4, half, block, block - 1, me + 1)
 
     def forward(block):
-        for half in (1, 0):
+        for half in (0, 1):
             on(exists(block), functools.partial(arrived, block, half))
+            if block == 2:
+                on(exists(block) & (depth > 0) & (depth < 7) & exists(-2), pass_on(half).start)
+                on(exists(block) & (core == 1), row_copy(3, half, block, 3, me - 1).start)
             on(exists(block) & (core == 0), to_next(block, half).start)
-            if block == 2:
-                on(exists(block) & (core == 1), row_copy(3, half, block, 3, me - 1).start)
 
     def catch_up():
-        def relay_late():
-            meet(1)
-            relay()
-
-        on((depth == 0) & exists(-2), relay_late)
-        on(exists(-4), lambda: meet(2))
+        meet(1)
         for half in (1, 0):
             @pl.when((half == 1) | jnp.logical_not(late))
             def _():
-                on((depth == 0) & exists(-2), to_two(half).start)
                 on(exists(-4), to_four(half).start)
+                to_two(half).start()
+
+        for half in (0, 1):
+            on(exists(2), pass_on(half).start)
 
     early = jnp.logical_not(late)
 
@@ -321,30 +319,31 @@
         def _():
             half = jnp.where((t == 1) | ((t == 0) & late), 1, 0)
             whiten(half)
+            on((t == 5) & exists(-4), to_four(half).start)
+            on(((depth > 0) | (t == 5)) & exists(-2), to_two(half).start)
             on(core == 1, to_sibling(half).start)
-            on(((depth > 0) | (t == 5)) & exists(-2), to_two(half).start)
-            on((depth > 1) & (t == 0) & exists(-4), lambda: meet(2))
-            on(((depth > 1) | (t == 5)) & exists(-4), to_four(half).start)
 
         @pl.when((t == 2) | ((t == 3) & early) | (t == 4) | ((t >= 6) & late))
         def _():
-            @pl.when(t == 2)
-            def _():
-                forward(2)
-                for half in (1, 0):
-                    on(exists(1), functools.partial(arrived, 1, half))
-                load_table.wait()
-
-            @pl.when(t == 4)
+            on(t == jnp.where(last & (core == 0), 4, 2), lambda: forward(2))
+
+            @pl.when(t == jnp.where(last, 2, jnp.where((core == 0) & early, 3, 4)))
             def _():
                 on(exists(-1) & late, send_left)
-                on(depth <= 1, catch_up)
+                on((depth == 0) & exists(-2), catch_up)
                 forward(4)
-                for half in (1, 0):
-                    on(exists(3), functools.partial(arrived, 3, half))
+
+            on(t == 2, load_table.wait)
+            pair = jnp.where((t == 4) | (t == 7), 1, 0)
+            pair = jnp.where(last, 1 - pair, pair)
+            for block in (1, 3):
+                for piece in (0, 1):
+                    on(
+                        ((t == 2) | (t == 4)) & (pair == block // 2) & exists(block),
+                        functools.partial(arrived, block, piece),
+                    )
 
             half = jnp.where((t == 2) | (t == 4), 1, 0)
-            pair = jnp.where((t == 4) | (t == 7), 1, 0)
             near_rows = pl.ds(pl.multiple_of(half * HALF, HALF), HALF)
             far_rows = pl.ds(pl.multiple_of(CH + pair * 2 * CH, CH), 2 * CH)
             part_ref[near_rows, pl.ds(pl.multiple_of(pair * 2 * CH, CH), 2 * CH), :] = correlate(
@@ -361,7 +360,8 @@
     for half in (1, 0):
         on(core == 1, to_sibling(half).wait_send)
         on(exists(-2), to_two(half).wait_send)
-        on(exists(-4), to_four(half).wait_send)
+        on(exists(2) & (depth < 7) & exists(-2), pass_on(half).wait_send)
+        on((depth == 0) & exists(-4), to_four(half).wait_send)
     for half in (1, 0):
         on(exists(2), to_next(2, half).wait_send)
         on(exists(4) & (core == 0), to_next(4, half).wait_send)
@@ -369,9 +369,12 @@
 
 def finish_kernel(rows_ref, part_ref, table_ref, out_ref, done, sem):
     me = lax.axis_index("fiber")
-    late = (lax.rem(me, 2) == 0) & (lax.rem(me // 2, 8) == 0)
+    depth = lax.rem(me // 2, 8)
+    late = (lax.rem(me, 2) == 0) & (depth == 0)
+    start = pl.multiple_of(jnp.where(depth == 7, 0, 2 * CH), 2 * CH)
     below, above = pl.ds(0, HALF), pl.ds(HALF, HALF)
-    first, second = pl.ds(0, 2 * CH), pl.ds(2 * CH, 2 * CH)
+    first, second = pl.ds(pl.multiple_of(2 * CH - start, 2 * CH), 2 * CH), pl.ds(start, 2 * CH)
+    far_rows = pl.ds(pl.multiple_of(CH + start, CH), 2 * CH)
     upper = pltpu.make_async_copy(part_ref.at[above], out_ref.at[above], sem.at[0])
     lower = pltpu.make_async_copy(part_ref.at[below, first], out_ref.at[below, first], sem.at[1])
     rest = pltpu.make_async_copy(done, out_ref.at[below, second], sem.at[2])
@@ -384,7 +387,7 @@
     def _():
         done[...] = correlate(
             lambda cols: rows_ref[below, cols].astype(jnp.float32),
-            lambda cols: rows_ref[3 * CH :, cols],
+            lambda cols: rows_ref[far_rows, cols],
             table_ref,
             (HALF, 2 * CH, LAGS),
         )
@@ -424,10 +427,10 @@
             pltpu.VMEM((8, 128), jnp.int32),
             pltpu.VMEM((CH, 2 * FB), jnp.float32),
             pltpu.SemaphoreType.DMA((5 + CHUNKS,)),
-            pltpu.SemaphoreType.REGULAR((3,)),
+            pltpu.SemaphoreType.REGULAR((2,)),
             pltpu.SemaphoreType.DMA((2, CHUNKS + 1)),
             pltpu.SemaphoreType.DMA((2, CHUNKS + 1)),
-            pltpu.SemaphoreType.DMA((5, 2)),
+            pltpu.SemaphoreType.DMA((6, 2)),
             pltpu.SemaphoreType.DMA((4, 2)),
         ],
         compiler_params=pltpu.CompilerParams(

time: 24.1 us -> 24.7 us (1.025)
  the two profiles are of different devices: /device:TPU:479 before, /device:TPU:57 now
where the time goes in v5:
time: 24.7 us; the launch traced here: 24.5 us
  Pallas kernels  24.5 us (99%)
    pallas_call x1, Pallas kernels, on_device(): pl.pallas_call(functools.partial(spectra_kernel, count), out_shape=(jax.S...  22.7 us
    pallas_call x1, Pallas kernels, on_device(): pl.pallas_call(finish_kernel, out_shape=jax.ShapeDtypeStruct((channels, R...  1.86 us

profile of v5, /device:TPU:57, one launch (start us, length us, event | category | flops | bytes accessed | tf_op | source)
XLA Modules:
  0.0 24.5 jit_solution(12614979406950380816)
XLA Ops:
  0.0 0.0 copy-start
  0.0 22.7 %spectra.1 = (bf16[160,1536]{1,0:T(8,128)(2,1)S(1)}, bf16[32,128,256]{2,1,0:T(8,128)(2,1)S(1)}) custom-call(f32[32,3000]{1,0:T(8,128)} %traces_hbm.1, s32[1,32]{1,0:T(1,128)} %bitcast.2, s32[1,32]{1,0:T(1,128)} %bitcast.3, bf16[3,2,256,512]{3,2,1,0:T(8,128)(2,1)} %constant.6.clone.base_hbm, f32[2,768]{1,0:T(2,128)} %constant.7.clone.twiddle_hbm, ...), custom_call_target="tpu_custom_call" | custom-call | tf_op jit(solution)/shard_map/spectra/pallas_call | solution.py:408
  22.7 0.0 copy-done
  22.7 1.9 %finish.1 = bf16[32,128,256]{2,1,0:T(8,128)(2,1)} custom-call(bf16[160,1536]{1,0:T(8,128)(2,1)S(1)} %get-tuple-element.7.rows_ref, bf16[32,128,256]{2,1,0:T(8,128)(2,1)S(1)} %get-tuple-element.8.part_ref, bf16[1536,256]{1,0:T(8,128)(2,1)S(1)} %copy-done), custom_call_target="tpu_custom_call" | custom-call | tf_op jit(solution)/shard_map/finish/pallas_call | solution.py:446
Async XLA Ops:
  0.0 22.7 %copy-start = (bf16[1536,256]{1,0:T(8,128)(2,1)S(1)}, bf16[1536,256]{1,0:T(8,128)(2,1)}, u32[]{:S(2)}) copy-start(bf16[1536,256]{1,0:T(8,128)(2,1)} %constant.8.clone.table_hbm.table_ref) | copy-start | bytes 2359300

commit v6 on v5

--- a/solution.py
+++ b/solution.py
@@ -110,7 +110,7 @@
 
     for step in (1, 2):
         on(exists(-step), functools.partial(signal, barrier, -step))
-    on((depth < 7) & exists(2), functools.partial(signal, barrier, 2))
+    on((depth < 6) & exists(2), functools.partial(signal, barrier, 2))
 
     small = [
         pltpu.make_async_copy(live_hbm, live, in_sem.at[0]),
@@ -127,13 +127,14 @@
         pl.semaphore_wait(here_sem.at[slot], 1)
 
     def greet():
-        awaited = (exists(1), exists(2), (depth > 0) & exists(-2))
+        awaited = (exists(1), exists(2), (depth > 0) & (depth < 7) & exists(-2))
         peers = sum(jnp.where(peer, 1, 0) for peer in awaited)
         on(peers > 0, lambda: pl.semaphore_wait(barrier, peers))
         on(exists(1), functools.partial(signal, here_sem.at[0], 1))
-        on((depth == 7) & exists(2), functools.partial(signal, here_sem.at[1], 2))
+        on((depth >= 6) & exists(2), functools.partial(signal, here_sem.at[1], 2))
 
     last = depth == 7
+    on(last, greet)
 
     whole[...] = jnp.zeros_like(whole)
     for load in small:
@@ -168,11 +169,7 @@
         first[s * CH : (s + 1) * CH, :] = top
         second[s * CH : (s + 1) * CH, :] = (piece - top.astype(jnp.float32)).astype(jnp.bfloat16)
 
-    def greet_first():
-        greet()
-        on(exists(1), halo(0, CHUNKS).start)
-
-    on(last, greet_first)
+    on(last & exists(1), halo(0, CHUNKS).start)
 
     def transform(c, carry):
         pltpu.make_async_copy(base_hbm.at[c], base.at[c], in_sem.at[4 + c]).wait()
@@ -203,6 +200,12 @@
             on(exists(1), halo(0, piece).start)
 
     on(jnp.logical_not(last), open_right)
+
+    def relay():
+        meet(1)
+        on((core == 0) & exists(2), functools.partial(signal, here_sem.at[2], 2))
+
+    on(last, relay)
 
     def send_left():
         meet(0)
@@ -293,24 +296,22 @@
     def to_next(block, half):
         return row_copy(3 if block == 2 else 4, half, block, block - 1, me + 1)
 
-    def forward(block):
-        for half in (0, 1):
-            on(exists(block), functools.partial(arrived, block, half))
-            if block == 2:
-                on(exists(block) & (depth > 0) & (depth < 7) & exists(-2), pass_on(half).start)
-                on(exists(block) & (core == 1), row_copy(3, half, block, 3, me - 1).start)
-            on(exists(block) & (core == 0), to_next(block, half).start)
+    last_low = last & (core == 0)
+
+    def passes(half):
+        return exists(2) & exists(-2) & jnp.logical_not(last_low & (half == 0))
+
+    def forward(block, half):
+        on(exists(block), functools.partial(arrived, block, half))
+        if block == 2:
+            on(passes(half), pass_on(half).start)
+            on(exists(block) & (core == 1), row_copy(3, half, block, 3, me - 1).start)
+        on(exists(block) & (core == 0), to_next(block, half).start)
 
     def catch_up():
         meet(1)
-        for half in (1, 0):
-            @pl.when((half == 1) | jnp.logical_not(late))
-            def _():
-                on(exists(-4), to_four(half).start)
-                to_two(half).start()
-
-        for half in (0, 1):
-            on(exists(2), pass_on(half).start)
+        to_two(1).start()
+        on(jnp.logical_not(late), to_two(0).start)
 
     early = jnp.logical_not(late)
 
@@ -319,19 +320,29 @@
         def _():
             half = jnp.where((t == 1) | ((t == 0) & late), 1, 0)
             whiten(half)
-            on((t == 5) & exists(-4), to_four(half).start)
             on(((depth > 0) | (t == 5)) & exists(-2), to_two(half).start)
             on(core == 1, to_sibling(half).start)
 
+            @pl.when((t == 5) & exists(-4))
+            def _():
+                meet(2)
+                to_four(half).start()
+
         @pl.when((t == 2) | ((t == 3) & early) | (t == 4) | ((t >= 6) & late))
         def _():
-            on(t == jnp.where(last & (core == 0), 4, 2), lambda: forward(2))
-
-            @pl.when(t == jnp.where(last, 2, jnp.where((core == 0) & early, 3, 4)))
+            @pl.when(t == 2)
             def _():
                 on(exists(-1) & late, send_left)
                 on((depth == 0) & exists(-2), catch_up)
-                forward(4)
+                on(jnp.logical_not(last_low), lambda: forward(2, 0))
+                forward(2, 1)
+
+            on((t == 4) & last_low, lambda: forward(2, 0))
+
+            @pl.when(t == jnp.where(last, 2, jnp.where((core == 0) & early, 3, 4)))
+            def _():
+                forward(4, 0)
+                forward(4, 1)
 
             on(t == 2, load_table.wait)
             pair = jnp.where((t == 4) | (t == 7), 1, 0)
@@ -360,8 +371,8 @@
     for half in (1, 0):
         on(core == 1, to_sibling(half).wait_send)
         on(exists(-2), to_two(half).wait_send)
-        on(exists(2) & (depth < 7) & exists(-2), pass_on(half).wait_send)
-        on((depth == 0) & exists(-4), to_four(half).wait_send)
+        on(passes(half), pass_on(half).wait_send)
+    on(late & exists(-4), to_four(0).wait_send)
     for half in (1, 0):
         on(exists(2), to_next(2, half).wait_send)
         on(exists(4) & (core == 0), to_next(4, half).wait_send)
@@ -427,7 +438,7 @@
             pltpu.VMEM((8, 128), jnp.int32),
             pltpu.VMEM((CH, 2 * FB), jnp.float32),
             pltpu.SemaphoreType.DMA((5 + CHUNKS,)),
-            pltpu.SemaphoreType.REGULAR((2,)),
+            pltpu.SemaphoreType.REGULAR((3,)),
             pltpu.SemaphoreType.DMA((2, CHUNKS + 1)),
             pltpu.SemaphoreType.DMA((2, CHUNKS + 1)),
             pltpu.SemaphoreType.DMA((6, 2)),

time: 24.7 us -> 22.7 us (0.919)
  the two profiles are of different devices: /device:TPU:57 before, /device:TPU:185 now
where the time goes in v6:
time: 22.7 us; the launch traced here: 22.6 us
  Pallas kernels  22.6 us (100%)
    pallas_call x1, Pallas kernels, on_device(): pl.pallas_call(functools.partial(spectra_kernel, count), out_shape=(jax.S...  20.7 us
    pallas_call x1, Pallas kernels, on_device(): pl.pallas_call(finish_kernel, out_shape=jax.ShapeDtypeStruct((channels, R...  1.86 us

profile of v6, /device:TPU:185, one launch (start us, length us, event | category | flops | bytes accessed | tf_op | source)
XLA Modules:
  0.0 22.6 jit_solution(2789406020390059095)
XLA Ops:
  0.0 0.0 copy-start
  0.0 20.7 %spectra.1 = (bf16[160,1536]{1,0:T(8,128)(2,1)S(1)}, bf16[32,128,256]{2,1,0:T(8,128)(2,1)S(1)}) custom-call(f32[32,3000]{1,0:T(8,128)} %traces_hbm.1, s32[1,32]{1,0:T(1,128)} %bitcast.2, s32[1,32]{1,0:T(1,128)} %bitcast.3, bf16[3,2,256,512]{3,2,1,0:T(8,128)(2,1)} %constant.6.clone.base_hbm, f32[2,768]{1,0:T(2,128)} %constant.7.clone.twiddle_hbm, ...), custom_call_target="tpu_custom_call" | custom-call | tf_op jit(solution)/shard_map/spectra/pallas_call | solution.py:419
  20.7 0.0 copy-done
  20.8 1.9 %finish.1 = bf16[32,128,256]{2,1,0:T(8,128)(2,1)} custom-call(bf16[160,1536]{1,0:T(8,128)(2,1)S(1)} %get-tuple-element.7.rows_ref, bf16[32,128,256]{2,1,0:T(8,128)(2,1)S(1)} %get-tuple-element.8.part_ref, bf16[1536,256]{1,0:T(8,128)(2,1)S(1)} %copy-done), custom_call_target="tpu_custom_call" | custom-call | tf_op jit(solution)/shard_map/finish/pallas_call | solution.py:457
Async XLA Ops:
  0.0 20.7 %copy-start = (bf16[1536,256]{1,0:T(8,128)(2,1)S(1)}, bf16[1536,256]{1,0:T(8,128)(2,1)}, u32[]{:S(2)}) copy-start(bf16[1536,256]{1,0:T(8,128)(2,1)} %constant.8.clone.table_hbm.table_ref) | copy-start | bytes 2359300

commit v7 on v6

--- a/solution.py
+++ b/solution.py
@@ -308,6 +308,14 @@
             on(exists(block) & (core == 1), row_copy(3, half, block, 3, me - 1).start)
         on(exists(block) & (core == 0), to_next(block, half).start)
 
+    def hand_over():
+        forward(4, 0)
+        forward(4, 1)
+
+    def take(block):
+        for half in (0, 1):
+            on(exists(block), functools.partial(arrived, block, half))
+
     def catch_up():
         meet(1)
         to_two(1).start()
@@ -328,33 +336,47 @@
                 meet(2)
                 to_four(half).start()
 
-        @pl.when((t == 2) | ((t == 3) & early) | (t == 4) | ((t >= 6) & late))
+        @pl.when((t >= 2) & early)
+        def _():
+            on((t == 2) & (depth == 0) & exists(-2), catch_up)
+            on((t == 2) & last_low, lambda: forward(2, 1))
+            turn = t - 2
+            low_order = jnp.where(last & (turn > 0), jnp.where(turn == 3, 2, turn + 2), turn + 1)
+            high_order = jnp.where(turn == 0, 2, jnp.where(turn == 1, 1, jnp.where(turn == 2, 4, 3)))
+            high_last = jnp.where(turn == 0, 2, jnp.where(turn == 1, 4, jnp.where(turn == 2, 3, 1)))
+            block = jnp.where(core == 0, low_order, jnp.where(last, high_last, high_order))
+            for one in (1, 3):
+                on(block == one, functools.partial(take, one))
+            on(block == 2, lambda: forward(2, 0))
+            on((block == 2) & jnp.logical_not(last_low), lambda: forward(2, 1))
+            on(block == 4, hand_over)
+            on(t == 2, load_table.wait)
+
+            @pl.when(t < 5)
+            def _():
+                far_rows = pl.ds(pl.multiple_of(block * CH, CH), CH)
+                part_ref[:, pl.ds(pl.multiple_of((block - 1) * CH, CH), CH), :] = correlate(
+                    lambda cols: own[:, cols], lambda cols: rows_ref[far_rows, cols], table, (CH, CH, LAGS)
+                )
+
+        @pl.when(((t == 2) | (t == 4) | (t >= 6)) & late)
         def _():
             @pl.when(t == 2)
             def _():
-                on(exists(-1) & late, send_left)
-                on((depth == 0) & exists(-2), catch_up)
-                on(jnp.logical_not(last_low), lambda: forward(2, 0))
+                on(exists(-1), send_left)
+                on(exists(-2), catch_up)
+                forward(2, 0)
                 forward(2, 1)
-
-            on((t == 4) & last_low, lambda: forward(2, 0))
-
-            @pl.when(t == jnp.where(last, 2, jnp.where((core == 0) & early, 3, 4)))
+                take(1)
+                load_table.wait()
+
+            @pl.when(t == 4)
             def _():
-                forward(4, 0)
-                forward(4, 1)
-
-            on(t == 2, load_table.wait)
+                hand_over()
+                take(3)
+
+            half = jnp.where(t <= 4, 1, 0)
             pair = jnp.where((t == 4) | (t == 7), 1, 0)
-            pair = jnp.where(last, 1 - pair, pair)
-            for block in (1, 3):
-                for piece in (0, 1):
-                    on(
-                        ((t == 2) | (t == 4)) & (pair == block // 2) & exists(block),
-                        functools.partial(arrived, block, piece),
-                    )
-
-            half = jnp.where((t == 2) | (t == 4), 1, 0)
             near_rows = pl.ds(pl.multiple_of(half * HALF, HALF), HALF)
             far_rows = pl.ds(pl.multiple_of(CH + pair * 2 * CH, CH), 2 * CH)
             part_ref[near_rows, pl.ds(pl.multiple_of(pair * 2 * CH, CH), 2 * CH), :] = correlate(
@@ -363,7 +385,7 @@
 
         return carry
 
-    lax.fori_loop(0, jnp.where(late, 8, 5), stage, 0)
+    lax.fori_loop(0, jnp.where(late, 8, 6), stage, 0)
 
     for side in (0, 1):
         for piece in range(CHUNKS + 1):
@@ -380,32 +402,34 @@
 
 def finish_kernel(rows_ref, part_ref, table_ref, out_ref, done, sem):
     me = lax.axis_index("fiber")
-    depth = lax.rem(me // 2, 8)
-    late = (lax.rem(me, 2) == 0) & (depth == 0)
-    start = pl.multiple_of(jnp.where(depth == 7, 0, 2 * CH), 2 * CH)
-    below, above = pl.ds(0, HALF), pl.ds(HALF, HALF)
-    first, second = pl.ds(pl.multiple_of(2 * CH - start, 2 * CH), 2 * CH), pl.ds(start, 2 * CH)
-    far_rows = pl.ds(pl.multiple_of(CH + start, CH), 2 * CH)
-    upper = pltpu.make_async_copy(part_ref.at[above], out_ref.at[above], sem.at[0])
-    lower = pltpu.make_async_copy(part_ref.at[below, first], out_ref.at[below, first], sem.at[1])
-    rest = pltpu.make_async_copy(done, out_ref.at[below, second], sem.at[2])
-    rest_there = pltpu.make_async_copy(part_ref.at[below, second], out_ref.at[below, second], sem.at[2])
-    upper.start()
-    lower.start()
-    pl.when(late)(rest_there.start)
+    core, depth = lax.rem(me, 2), lax.rem(me // 2, 8)
+    late = (core == 0) & (depth == 0)
+    block = jnp.where(depth == 7, 1, 3) - core
+
+    def place(step):
+        return pl.ds(pl.multiple_of(lax.rem(block + step, REACH) * CH, CH), CH)
+
+    def there(step):
+        return pltpu.make_async_copy(part_ref.at[:, place(step)], out_ref.at[:, place(step)], sem.at[step])
+
+    for step in range(1, REACH):
+        there(step).start()
+    pl.when(late)(there(0).start)
+    rest = pltpu.make_async_copy(done, out_ref.at[:, place(0)], sem.at[0])
 
     @pl.when(jnp.logical_not(late))
     def _():
+        far_rows = pl.ds(pl.multiple_of((block + 1) * CH, CH), CH)
         done[...] = correlate(
-            lambda cols: rows_ref[below, cols].astype(jnp.float32),
+            lambda cols: rows_ref[0:CH, cols].astype(jnp.float32),
             lambda cols: rows_ref[far_rows, cols],
             table_ref,
-            (HALF, 2 * CH, LAGS),
+            (CH, CH, LAGS),
         )
         rest.start()
 
-    upper.wait()
-    lower.wait()
+    for step in range(1, REACH):
+        there(step).wait()
     rest.wait()
 
 
@@ -460,8 +484,8 @@
         in_specs=[in_vmem] * 3,
         out_specs=in_hbm,
         scratch_shapes=[
-            pltpu.VMEM((HALF, 2 * CH, LAGS), jnp.bfloat16),
-            pltpu.SemaphoreType.DMA((3,)),
+            pltpu.VMEM((CH, CH, LAGS), jnp.bfloat16),
+            pltpu.SemaphoreType.DMA((REACH,)),
         ],
         compiler_params=pltpu.CompilerParams(vmem_limit_bytes=40 * 1024 * 1024),
         name="finish",

time: 22.7 us -> 21.9 us (0.965)
  the two profiles are of different devices: /device:TPU:185 before, /device:TPU:1 now
where the time goes in v7:
time: 21.9 us; the launch traced here: 21.6 us
  Pallas kernels  21.6 us (99%)
    pallas_call x1, Pallas kernels, on_device(): pl.pallas_call(functools.partial(spectra_kernel, count), out_shape=(jax.S...  19.7 us
    pallas_call x1, Pallas kernels, on_device(): pl.pallas_call(finish_kernel, out_shape=jax.ShapeDtypeStruct((channels, R...  1.92 us

profile of v7, /device:TPU:1, one launch (start us, length us, event | category | flops | bytes accessed | tf_op | source)
XLA Modules:
  0.0 21.6 jit_solution(4822668455006834957)
XLA Ops:
  0.0 0.0 copy-start
  0.0 19.7 %spectra.1 = (bf16[160,1536]{1,0:T(8,128)(2,1)S(1)}, bf16[32,128,256]{2,1,0:T(8,128)(2,1)S(1)}) custom-call(f32[32,3000]{1,0:T(8,128)} %traces_hbm.1, s32[1,32]{1,0:T(1,128)} %bitcast.2, s32[1,32]{1,0:T(1,128)} %bitcast.3, bf16[3,2,256,512]{3,2,1,0:T(8,128)(2,1)} %constant.6.clone.base_hbm, f32[2,768]{1,0:T(2,128)} %constant.7.clone.twiddle_hbm, ...), custom_call_target="tpu_custom_call" | custom-call | tf_op jit(solution)/shard_map/spectra/pallas_call | solution.py:443
  19.7 0.0 copy-done
  19.7 1.9 %finish.1 = bf16[32,128,256]{2,1,0:T(8,128)(2,1)} custom-call(bf16[160,1536]{1,0:T(8,128)(2,1)S(1)} %get-tuple-element.7.rows_ref, bf16[32,128,256]{2,1,0:T(8,128)(2,1)S(1)} %get-tuple-element.8.part_ref, bf16[1536,256]{1,0:T(8,128)(2,1)S(1)} %copy-done), custom_call_target="tpu_custom_call" | custom-call | tf_op jit(solution)/shard_map/finish/pallas_call | solution.py:481
Async XLA Ops:
  0.0 19.7 %copy-start = (bf16[1536,256]{1,0:T(8,128)(2,1)S(1)}, bf16[1536,256]{1,0:T(8,128)(2,1)}, u32[]{:S(2)}) copy-start(bf16[1536,256]{1,0:T(8,128)(2,1)} %constant.8.clone.table_hbm.table_ref) | copy-start | bytes 2359300

commit v8 on v7

--- a/solution.py
+++ b/solution.py
@@ -247,9 +247,8 @@
 
         @pl.when(there)
         def _():
-            for piece in (CHUNKS, *range(CHUNKS)):
-                on(half == 0, halo(0, piece).wait_recv)
-                on(half == 1, halo(1, piece).wait_recv)
+            on(half == 0, halo(0, CHUNKS).wait_recv)
+            on(half == 1, halo(1, CHUNKS).wait_recv)
 
         @pl.when(jnp.logical_not(there))
         def _():
@@ -266,6 +265,14 @@
         alive = (mine & 1).astype(jnp.float32)
         weights = jnp.where(half == 1, pltpu.roll(inside, 128 - HALF, 1), inside)[:, : 3 * HALF].astype(jnp.bfloat16)
         weights = jnp.concatenate([weights, weights, weights], axis=1)
+        share = alive / divisor
+
+        @pl.when(there)
+        def _():
+            for piece in range(CHUNKS):
+                on(half == 0, halo(0, piece).wait_recv)
+                on(half == 1, halo(1, piece).wait_recv)
+
         same = jnp.where(band_row == band_col, 1.0, 0.0).astype(jnp.bfloat16)
         for c in range(CHUNKS):
             parts = []
@@ -274,10 +281,10 @@
                 stack = jnp.concatenate(split3(spec[pl.ds(low, 3 * HALF), cols]), axis=0)
                 sums = dot(weights, stack)
                 value = spec[pl.ds(pl.multiple_of(HALF + low, HALF), HALF), cols]
-                parts.append(alive * (value * alive - sums / divisor))
+                parts.append(value * alive - sums * share)
             square = parts[0] * parts[0] + parts[1] * parts[1]
-            sums = dot(jnp.concatenate(split3(square), axis=0), same)
-            power = (sums[:HALF] + (sums[HALF : 2 * HALF] + sums[2 * HALF :])) * (1.0 / BAND)
+            sums = dot(jnp.concatenate(split3(square)[:2], axis=0), same)
+            power = (sums[:HALF] + sums[HALF:]) * (1.0 / BAND)
             scale = lax.rsqrt(power + WHITEN_EPS)
             for part, offset in zip(parts, (c * WIDE, c * WIDE + CHUNK)):
                 white = (part * scale).astype(jnp.bfloat16)

time: 21.9 us -> 21.7 us (level)
  no operation moved by 1% of the time
where the time goes in v8:
time: 21.7 us; the launch traced here: 21.4 us
  Pallas kernels  21.4 us (99%)
    pallas_call x1, Pallas kernels, on_device(): pl.pallas_call(functools.partial(spectra_kernel, count), out_shape=(jax.S...  19.5 us
    pallas_call x1, Pallas kernels, on_device(): pl.pallas_call(finish_kernel, out_shape=jax.ShapeDtypeStruct((channels, R...  1.92 us

profile of v8, /device:TPU:1, one launch (start us, length us, event | category | flops | bytes accessed | tf_op | source)
XLA Modules:
  0.0 21.4 jit_solution(16751965414915272662)
XLA Ops:
  0.0 0.0 copy-start
  0.0 19.5 %spectra.1 = (bf16[160,1536]{1,0:T(8,128)(2,1)S(1)}, bf16[32,128,256]{2,1,0:T(8,128)(2,1)S(1)}) custom-call(f32[32,3000]{1,0:T(8,128)} %traces_hbm.1, s32[1,32]{1,0:T(1,128)} %bitcast.2, s32[1,32]{1,0:T(1,128)} %bitcast.3, bf16[3,2,256,512]{3,2,1,0:T(8,128)(2,1)} %constant.6.clone.base_hbm, f32[2,768]{1,0:T(2,128)} %constant.7.clone.twiddle_hbm, ...), custom_call_target="tpu_custom_call" | custom-call | tf_op jit(solution)/shard_map/spectra/pallas_call | solution.py:450
  19.5 0.0 copy-done
  19.5 1.9 %finish.1 = bf16[32,128,256]{2,1,0:T(8,128)(2,1)} custom-call(bf16[160,1536]{1,0:T(8,128)(2,1)S(1)} %get-tuple-element.7.rows_ref, bf16[32,128,256]{2,1,0:T(8,128)(2,1)S(1)} %get-tuple-element.8.part_ref, bf16[1536,256]{1,0:T(8,128)(2,1)S(1)} %copy-done), custom_call_target="tpu_custom_call" | custom-call | tf_op jit(solution)/shard_map/finish/pallas_call | solution.py:488
Async XLA Ops:
  0.0 19.5 %copy-start = (bf16[1536,256]{1,0:T(8,128)(2,1)S(1)}, bf16[1536,256]{1,0:T(8,128)(2,1)}, u32[]{:S(2)}) copy-start(bf16[1536,256]{1,0:T(8,128)(2,1)} %constant.8.clone.table_hbm.table_ref) | copy-start | bytes 2359300
